TPU v7x, 512 devices: a whole 4x8x8 slice. The times are simulated.
512 devices in a mesh: segment: 32 (over y, z_hi), tp: 16 (over x, z_lo, core).
Axes of the slice: x: 4, y: 8, z: 8 (z_hi: 4, z_lo: 2; z = z_hi * 2 + z_lo), core: 2. Of those that a mesh axis runs over, the one named last changes fastest.
Arguments:
- residual: bfloat16 [32, 128, 4096], P('segment', 'tp'), may hold values from -6 to 6
- pending: bfloat16 [32, 128, 4096], P('segment', 'tp'), may hold values from -6 to 6
- span_index: int32 [32], P('segment'), may hold values from 0 to 63
- prefix_len: int32 [32], P('segment'), may hold values from 192 to 1536
- norm_gain: bfloat16 [32, 4096], P('segment'), may hold values from 0.099609375 to 1.8984375
- w_query: bfloat16 [32, 4096, 4096], P('segment', None, 'tp'), may hold values from -0.1875 to 0.1875
- w_kv: bfloat16 [32, 4096, 1024], P('segment', None, 'tp'), may hold values from -0.09375 to 0.09375
- w_out: bfloat16 [32, 4096, 4096], P('segment', 'tp'), may hold values from -0.5 to 0.5
- prefix_cache: bfloat16 [32, 6144, 256], P('segment', 'tp'), may hold values from -68 to 68
Outputs:
- carried: bfloat16 [32, 128, 4096], P('segment', 'tp')
- output: bfloat16 [32, 128, 4096], P('segment', 'tp')
All inputs are finite; a program needn't handle non-finite values.
Results may differ from a plain program's by a relative error of at most 0.04.
Values may be sent and summed in bfloat16 or wider, within the bound.
No kernel may reach another device: no remote copies, remote signals or barrier semaphores. Data moves between devices by JAX's collectives and lax.ppermute only.
A program may use at most 64 MiB of HBM per device.

v0:
```python
import jax
import jax.numpy as jnp
from jax import lax
from jax.sharding import PartitionSpec as P

KV_HEADS = 4
HD = 128
SPAN = 128
PREFIX = 1536
TICKS = 2


norm_eps = 1e-05
rope_base = 500000.0


def from_partner(array, axis, stride):
    return lax.ppermute(array, axis, [(i, i ^ 1 << stride) for i in range(lax.axis_size(axis))])


def shifted(block, axis, distance):
    devices = range(lax.axis_size(axis))
    route = [(i - distance, i) for i in devices if i - distance in devices]
    return lax.ppermute(block, axis, route)


def rotate(values, positions):
    half_width = values.shape[-1] // 2
    inverse = rope_base ** (
        -jnp.arange(0, values.shape[-1], 2, dtype=jnp.float32) / values.shape[-1]
    )
    angles = positions.astype(jnp.float32)[:, None] * inverse[None, :]
    cosine_table = jnp.cos(angles)[:, None, :]
    sine_table = jnp.sin(angles)[:, None, :]
    first_half = values[..., :half_width]
    second_half = values[..., half_width:]
    return jnp.concatenate(
        [
            first_half * cosine_table - second_half * sine_table,
            second_half * cosine_table + first_half * sine_table,
        ],
        axis=-1,
    )


def shards(
    residual, pending, span_index, prefix_len, norm_gain, w_query, w_kv, w_out, prefix_cache
):
    group_size = lax.axis_size("tp") // KV_HEADS
    group_bits = group_size.bit_length() - 1
    tp_place = lax.axis_index("tp")
    local_heads = w_query.shape[2] // HD
    weight_query = w_query[0]
    weight_pairs = w_kv[0]
    weight_out = w_out[0]
    query_width = weight_query.shape[1]
    gain_row = norm_gain[0].astype(jnp.float32)
    head_cache = prefix_cache[0]
    for bit_number in range(group_bits):
        partner = from_partner(head_cache, "tp", bit_number)
        lower_half = tp_place // (1 << bit_number) % 2 == 0
        head_cache = jnp.where(
            lower_half,
            jnp.concatenate([head_cache, partner], 0),
            jnp.concatenate([partner, head_cache], 0),
        )
    cache_keys = head_cache[:, :HD]
    cache_values = head_cache[:, HD:]
    slot_index = jnp.arange(PREFIX, dtype=jnp.int32)
    token_index = jnp.arange(SPAN, dtype=jnp.int32)
    causal = token_index[None, :] <= token_index[:, None]
    score_scale = HD ** (-0.5)
    rows_now = residual[0]
    pending_now = pending[0]
    index_now = span_index
    for segment_tick in range(TICKS):
        last_tick = segment_tick + 1 == TICKS
        widths = rows_now.astype(jnp.float32)
        mean_square = jnp.mean(widths * widths, axis=-1, keepdims=True)
        normed = (widths * lax.rsqrt(mean_square + norm_eps) * gain_row).astype(jnp.bfloat16)
        carried = (widths + pending_now.astype(jnp.float32)).astype(jnp.bfloat16)
        block_rows = lax.all_gather(normed, "tp", axis=0, tiled=True)
        projected = jnp.concatenate(
            [
                jnp.dot(block_rows, weight_query, preferred_element_type=jnp.float32),
                jnp.dot(block_rows, weight_pairs, preferred_element_type=jnp.float32),
            ],
            axis=1,
        )
        positions = index_now[0] * SPAN + token_index
        queries = rotate(
            projected[:, :query_width].reshape(SPAN, local_heads, HD), positions
        ).astype(jnp.bfloat16)
        fresh_head = projected[:, query_width:].astype(jnp.bfloat16)
        for bit_number in range(group_bits):
            partner = from_partner(fresh_head, "tp", bit_number)
            lower_half = tp_place // (1 << bit_number) % 2 == 0
            fresh_head = jnp.where(
                lower_half,
                jnp.concatenate([fresh_head, partner], 1),
                jnp.concatenate([partner, fresh_head], 1),
            )
        new_keys = rotate(fresh_head[:, None, :HD].astype(jnp.float32), positions)[:, 0, :].astype(
            jnp.bfloat16
        )
        new_values = fresh_head[:, HD:]
        score_prefix = (
            jnp.einsum("chd,pd->hcp", queries, cache_keys, preferred_element_type=jnp.float32)
            * score_scale
        )
        score_span = (
            jnp.einsum("chd,kd->hck", queries, new_keys, preferred_element_type=jnp.float32)
            * score_scale
        )
        score_prefix = jnp.where(
            (slot_index < prefix_len[0])[None, None, :], score_prefix, -jnp.inf
        )
        score_span = jnp.where(causal[None], score_span, -jnp.inf)
        row_peak = jnp.maximum(
            jnp.max(score_prefix, axis=-1, keepdims=True),
            jnp.max(score_span, axis=-1, keepdims=True),
        )
        exp_prefix = jnp.exp(score_prefix - row_peak)
        exp_span = jnp.exp(score_span - row_peak)
        denominator = jnp.sum(exp_prefix, axis=-1, keepdims=True) + jnp.sum(
            exp_span, axis=-1, keepdims=True
        )
        weight_prefix = (exp_prefix / denominator).astype(jnp.bfloat16)
        weight_span = (exp_span / denominator).astype(jnp.bfloat16)
        attended = jnp.einsum(
            "hcp,pd->chd", weight_prefix, cache_values, preferred_element_type=jnp.float32
        )
        attended = attended + jnp.einsum(
            "hck,kd->chd", weight_span, new_values, preferred_element_type=jnp.float32
        )
        attended = attended.astype(jnp.bfloat16).reshape(SPAN, local_heads * HD)
        summed = lax.psum_scatter(
            jnp.dot(attended, weight_out, preferred_element_type=jnp.float32),
            "tp",
            scatter_dimension=0,
            tiled=True,
        )
        output = summed.astype(jnp.bfloat16)
        if not last_tick:
            rows_now, pending_now, index_now = shifted((carried, output, index_now), "segment", 1)
    return (carried[None], output[None])


def solution(mesh):
    in_specs = (
        P("segment", "tp", None),
        P("segment", "tp", None),
        P("segment"),
        P("segment"),
        P("segment", None),
        P("segment", None, "tp"),
        P("segment", None, "tp"),
        P("segment", "tp", None),
        P("segment", "tp", None),
    )
    out_specs = (P("segment", "tp", None), P("segment", "tp", None))
    return jax.shard_map(shards, mesh=mesh, in_specs=in_specs, out_specs=out_specs, check_vma=False)
```

profile of v0, /device:TPU:24, one launch (start us, length us, event | category | flops | bytes accessed | tf_op | source)
XLA Modules:
  0.0 278.5 jit_solution(12235251727434723015)
XLA Ops:
  10.8 6.1 %collective-permute-start.6 = (s32[1]{0:T(128)}, s32[1]{0:T(128)}, u32[]{:S(2)}, u32[]{:S(2)}) collective-permute-start(s32[1]{0:T(128)} %param.11), channel_id=1, source_target_pairs={{0,16},{16,32},{32,48},{48,64},{64,80},{80,96},{96,112},{112,128},... | collective-permute-start | bytes 20 | tf_op jit(solution)/shard_map/ppermute | solution.py:24
  16.9 1.9 collective-permute-start.1
  23.0 4.3 %collective-permute-start.2 = (bf16[768,256]{1,0:T(8,128)(2,1)S(1)}, bf16[768,256]{1,0:T(8,128)(2,1)S(1)}, u32[]{:S(2)}, u32[]{:S(2)}) collective-permute-start(bf16[768,256]{1,0:T(8,128)(2,1)S(1)} %maximum_select_fusion.1), channel_id=1, source_target_pairs={{0,2},{1,3},{2,0},{3,1},{4,6},{5,7},{6,4},{7,5},{8,10},{9,11},{10,... | collective-permute-start | bytes 1179656 | tf_op jit(solution)/shard_map/ppermute | solution.py:18
  27.9 4.1 %copy.41 = bf16[256,4096]{1,0:T(8,128)(2,1)} copy(bf16[256,4096]{0,1:T(8,128)(2,1)} %bitcast.107) | data formatting | bytes 4194304 | tf_op jit(solution)/shard_map/dot_general | solution.py:85
  34.2 4.6 %collective-permute-done.2 = bf16[768,256]{1,0:T(8,128)(2,1)S(1)} collective-permute-done((bf16[768,256]{1,0:T(8,128)(2,1)S(1)}, bf16[768,256]{1,0:T(8,128)(2,1)S(1)}, u32[]{:S(2)}, u32[]{:S(2)}) %collective-permute-start.2) | collective-permute-done | bytes 393248 | tf_op jit(solution)/shard_map/ppermute | solution.py:18
  40.0 13.9 %all-gather.3.cloned.1.call-done = bf16[128,4096]{1,0:T(8,128)(2,1)} async-done(((bf16[8,4096]{1,0:T(8,128)(2,1)}), bf16[128,4096]{1,0:T(8,128)(2,1)}) %all-gather.3.cloned.1.call-update) | async-done | bytes 1048592 | tf_op jit(solution)/shard_map/all_gather | solution.py:82
  53.9 1.8 convolution_convert_fusion.1
  55.7 2.2 collective-permute-start.3
  57.9 2.4 fusion.18
  60.4 2.6 collective-permute-start.4
  63.4 2.8 collective-permute-done.4
  67.6 1.8 fusion.6
  69.5 4.5 %collective-permute-start = (bf16[8,4096]{1,0:T(8,128)(2,1)}, bf16[8,4096]{1,0:T(8,128)(2,1)S(1)}, u32[]{:S(2)}, u32[]{:S(2)}) collective-permute-start(bf16[8,4096]{1,0:T(8,128)(2,1)} %get-tuple-element.12), channel_id=1, source_target_pairs={{0,16},{16,32},{32,48},{48,64},{64,80},{80,96},{96,112},{112,128},... | collective-permute-start | bytes 196616 | tf_op jit(solution)/shard_map/ppermute | solution.py:24
  74.0 5.0 %collective-permute-done = bf16[8,4096]{1,0:T(8,128)(2,1)S(1)} collective-permute-done((bf16[8,4096]{1,0:T(8,128)(2,1)}, bf16[8,4096]{1,0:T(8,128)(2,1)S(1)}, u32[]{:S(2)}, u32[]{:S(2)}) %collective-permute-start) | collective-permute-done | bytes 65568 | tf_op jit(solution)/shard_map/ppermute | solution.py:24
  79.6 59.4 %reduce-scatter.3.cloned.1.call-done = f32[8,4096]{1,0:T(8,128)} async-done(((f32[128,4096]{1,0:T(8,128)}), f32[8,4096]{1,0:T(8,128)}) %reduce-scatter.3.cloned.1.call-update) | async-done | bytes 131088 | tf_op jit(solution)/shard_map/reduce_scatter | solution.py:137
  140.0 4.6 %collective-permute-start.5 = (bf16[8,4096]{1,0:T(8,128)(2,1)S(1)}, bf16[8,4096]{1,0:T(8,128)(2,1)S(1)}, u32[]{:S(2)}, u32[]{:S(2)}) collective-permute-start(bf16[8,4096]{1,0:T(8,128)(2,1)S(1)} %convert_element_type.122), channel_id=1, source_target_pairs={{0,16},{16,32},{32,48},{48,64},{64,80},{80,96},{96,112},{112,128},... | collective-permute-start | bytes 196616 | tf_op jit(solution)/shard_map/ppermute | solution.py:24
  145.3 3.9 %collective-permute-done.5 = bf16[8,4096]{1,0:T(8,128)(2,1)S(1)} collective-permute-done((bf16[8,4096]{1,0:T(8,128)(2,1)S(1)}, bf16[8,4096]{1,0:T(8,128)(2,1)S(1)}, u32[]{:S(2)}, u32[]{:S(2)}) %collective-permute-start.5) | collective-permute-done | bytes 65568 | tf_op jit(solution)/shard_map/ppermute | solution.py:24
  149.9 35.1 %all-gather.5.cloned.1.call-done = bf16[128,4096]{1,0:T(8,128)(2,1)} async-done(((bf16[8,4096]{1,0:T(8,128)(2,1)}), bf16[128,4096]{1,0:T(8,128)(2,1)}) %all-gather.5.cloned.1.call-update) | async-done | bytes 1048592 | tf_op jit(solution)/shard_map/all_gather | solution.py:82
  186.8 2.1 collective-permute-start.7
  189.0 2.3 fusion.16
  191.4 3.1 %collective-permute-start.8 = (bf16[128,128]{0,1:T(8,128)(2,1)S(1)}, bf16[128,128]{0,1:T(8,128)(2,1)S(1)}, u32[]{:S(2)}, u32[]{:S(2)}) collective-permute-start(bf16[128,128]{0,1:T(8,128)(2,1)S(1)} %maximum_select_fusion.5), channel_id=1, source_target_pairs={{0,2},{1,3},{2,0},{3,1},{4,6},{5,7},{6,4},{7,5},{8,10},{9,11},{10,... | collective-permute-start | bytes 98312 | tf_op jit(solution)/shard_map/ppermute | solution.py:18
  194.9 2.3 collective-permute-done.8
  198.6 1.8 fusion.4
  200.4 70.0 %reduce-scatter.5.cloned.1.call-done = f32[8,4096]{1,0:T(8,128)} async-done(((f32[128,4096]{1,0:T(8,128)}), f32[8,4096]{1,0:T(8,128)}) %reduce-scatter.5.cloned.1.call-update) | async-done | bytes 131088 | tf_op jit(solution)/shard_map/reduce_scatter | solution.py:137
  (84 shorter events, 19.9 us)
Async XLA Ops:
  7.2 60.4 %copy-start = (bf16[1,256,4096]{2,1,0:T(8,128)(2,1)S(1)}, bf16[1,256,4096]{2,1,0:T(8,128)(2,1)}, u32[]{:S(2)}) copy-start(bf16[1,256,4096]{2,1,0:T(8,128)(2,1)} %param.16) | copy-start | bytes 6291460
  7.2 46.7 %all-gather.3.cloned.1.call-start = ((), (), s32[]{:S(2)}) async-start(), calls=%async_computation.2 | async-start | bytes 1114112 | tf_op jit(solution)/shard_map/all_gather | solution.py:82
  10.7 128.4 %reduce-scatter.3.cloned.1.call-start = ((), (), s32[]{:S(2)}) async-start(), calls=%async_computation.3 | async-start | bytes 2228224 | tf_op jit(solution)/shard_map/reduce_scatter | solution.py:137
  10.8 21.3 %collective-permute-start.6 = (s32[1]{0:T(128)}, s32[1]{0:T(128)}, u32[]{:S(2)}, u32[]{:S(2)}) collective-permute-start(s32[1]{0:T(128)} %param.11), channel_id=1, source_target_pairs={{0,16},{16,32},{32,48},{48,64},{64,80},{80,96},{96,112},{112,128},... | collective-permute-start | bytes 20 | tf_op jit(solution)/shard_map/ppermute | solution.py:24
  16.9 5.0 %collective-permute-start.1 = (bf16[384,256]{1,0:T(8,128)(2,1)}, bf16[384,256]{1,0:T(8,128)(2,1)S(1)}, u32[]{:S(2)}, u32[]{:S(2)}) collective-permute-start(bf16[384,256]{1,0:T(8,128)(2,1)} %bitcast.108), channel_id=1, source_target_pairs={{0,1},{1,0},{2,3},{3,2},{4,5},{5,4},{6,7},{7,6},{8,9},{9,8},{10,11... | collective-permute-start | bytes 589832 | tf_op jit(solution)/shard_map/ppermute | solution.py:18
  23.0 15.8 %collective-permute-start.2 = (bf16[768,256]{1,0:T(8,128)(2,1)S(1)}, bf16[768,256]{1,0:T(8,128)(2,1)S(1)}, u32[]{:S(2)}, u32[]{:S(2)}) collective-permute-start(bf16[768,256]{1,0:T(8,128)(2,1)S(1)} %maximum_select_fusion.1), channel_id=1, source_target_pairs={{0,2},{1,3},{2,0},{3,1},{4,6},{5,7},{6,4},{7,5},{8,10},{9,11},{10,... | collective-permute-start | bytes 1179656 | tf_op jit(solution)/shard_map/ppermute | solution.py:18
  32.0 21.9 %copy-start.3 = (bf16[1,4096,64]{1,2,0:T(8,128)(2,1)S(1)}, bf16[1,4096,64]{1,2,0:T(8,128)(2,1)}, u32[]{:S(2)}) copy-start(bf16[1,4096,64]{1,2,0:T(8,128)(2,1)} %param.15) | copy-start | bytes 1572868
  55.7 4.6 %collective-permute-start.3 = (bf16[128,64]{0,1:T(8,128)(2,1)S(1)}, bf16[128,64]{0,1:T(8,128)(2,1)S(1)}, u32[]{:S(2)}, u32[]{:S(2)}) collective-permute-start(bf16[128,64]{0,1:T(8,128)(2,1)S(1)} %convolution_convert_fusion.1), channel_id=1, source_target_pairs={{0,1},{1,0},{2,3},{3,2},{4,5},{5,4},{6,7},{7,6},{8,9},{9,8},{10,11... | collective-permute-start | bytes 49160 | tf_op jit(solution)/shard_map/ppermute | solution.py:18
  57.9 5.1 %copy-start.4 = (bf16[1536,256]{1,0:T(8,128)(2,1)S(1)}, bf16[1536,256]{1,0:T(8,128)(2,1)}, u32[]{:S(2)}) copy-start(bf16[1536,256]{1,0:T(8,128)(2,1)} %maximum_select_fusion) | copy-start | bytes 2359300
  57.9 5.1 %copy-start.12 = (pred[1536]{0:T(1024)(128)(4,1)S(1)}, pred[1536]{0:T(1024)(128)(4,1)}, u32[]{:S(2)}) copy-start(pred[1536]{0:T(1024)(128)(4,1)} %iota_compare_fusion.1) | copy-start | bytes 4612
  60.3 5.9 %copy-start.7 = (f32[64]{0:T(128)S(1)}, f32[64]{0:T(128)}, u32[]{:S(2)}) copy-start(f32[64]{0:T(128)} %multiply_power_fusion) | copy-start | bytes 772
  60.3 5.9 %copy-start.11 = (f32[128]{0:T(128)S(1)}, f32[128]{0:T(128)}, u32[]{:S(2)}) copy-start(f32[128]{0:T(128)} %add_convert_fusion.3) | copy-start | bytes 1540
  60.3 6.1 %copy-start.5 = (pred[128,128]{0,1:T(8,128)(4,1)S(1)}, pred[128,128]{0,1:T(8,128)(4,1)}, u32[]{:S(2)}) copy-start(pred[128,128]{0,1:T(8,128)(4,1)} %iota_compare_fusion) | copy-start | bytes 49156
  60.4 5.8 %collective-permute-start.4 = (bf16[128,128]{0,1:T(8,128)(2,1)S(1)}, bf16[128,128]{0,1:T(8,128)(2,1)S(1)}, u32[]{:S(2)}, u32[]{:S(2)}) collective-permute-start(bf16[128,128]{0,1:T(8,128)(2,1)S(1)} %maximum_select_fusion.4), channel_id=1, source_target_pairs={{0,2},{1,3},{2,0},{3,1},{4,6},{5,7},{6,4},{7,5},{8,10},{9,11},{10,... | collective-permute-start | bytes 98312 | tf_op jit(solution)/shard_map/ppermute | solution.py:18
  69.4 115.6 %all-gather.5.cloned.1.call-start = ((), (), s32[]{:S(2)}) async-start(), calls=%async_computation.4 | async-start | bytes 1114112 | tf_op jit(solution)/shard_map/all_gather | solution.py:82
  69.5 9.5 %collective-permute-start = (bf16[8,4096]{1,0:T(8,128)(2,1)}, bf16[8,4096]{1,0:T(8,128)(2,1)S(1)}, u32[]{:S(2)}, u32[]{:S(2)}) collective-permute-start(bf16[8,4096]{1,0:T(8,128)(2,1)} %get-tuple-element.12), channel_id=1, source_target_pairs={{0,16},{16,32},{32,48},{48,64},{64,80},{80,96},{96,112},{112,128},... | collective-permute-start | bytes 196616 | tf_op jit(solution)/shard_map/ppermute | solution.py:24
  140.0 9.2 %collective-permute-start.5 = (bf16[8,4096]{1,0:T(8,128)(2,1)S(1)}, bf16[8,4096]{1,0:T(8,128)(2,1)S(1)}, u32[]{:S(2)}, u32[]{:S(2)}) collective-permute-start(bf16[8,4096]{1,0:T(8,128)(2,1)S(1)} %convert_element_type.122), channel_id=1, source_target_pairs={{0,16},{16,32},{32,48},{48,64},{64,80},{80,96},{96,112},{112,128},... | collective-permute-start | bytes 196616 | tf_op jit(solution)/shard_map/ppermute | solution.py:24
  149.9 120.6 %reduce-scatter.5.cloned.1.call-start = ((), (), s32[]{:S(2)}) async-start(), calls=%async_computation.5 | async-start | bytes 2228224 | tf_op jit(solution)/shard_map/reduce_scatter | solution.py:137
  186.8 7.6 %copy-start.13 = (pred[1536]{0:T(1024)(128)(4,1)S(1)}, pred[1536]{0:T(1024)(128)(4,1)}, u32[]{:S(2)}) copy-start(pred[1536]{0:T(1024)(128)(4,1)} %iota_compare_fusion.1) | copy-start | bytes 4612
  186.8 4.5 %collective-permute-start.7 = (bf16[128,64]{0,1:T(8,128)(2,1)S(1)}, bf16[128,64]{0,1:T(8,128)(2,1)S(1)}, u32[]{:S(2)}, u32[]{:S(2)}) collective-permute-start(bf16[128,64]{0,1:T(8,128)(2,1)S(1)} %convolution_convert_fusion), channel_id=1, source_target_pairs={{0,1},{1,0},{2,3},{3,2},{4,5},{5,4},{6,7},{7,6},{8,9},{9,8},{10,11... | collective-permute-start | bytes 49160 | tf_op jit(solution)/shard_map/ppermute | solution.py:18
  191.3 5.9 %copy-start.8 = (f32[64]{0:T(128)S(1)}, f32[64]{0:T(128)}, u32[]{:S(2)}) copy-start(f32[64]{0:T(128)} %multiply_power_fusion) | copy-start | bytes 772
  191.3 5.9 %copy-start.10 = (f32[128]{0:T(128)S(1)}, f32[128]{0:T(128)}, u32[]{:S(2)}) copy-start(f32[128]{0:T(128)} %copy-done.9) | copy-start | bytes 1540
  191.3 6.1 %copy-start.6 = (pred[128,128]{0,1:T(8,128)(4,1)S(1)}, pred[128,128]{0,1:T(8,128)(4,1)}, u32[]{:S(2)}) copy-start(pred[128,128]{0,1:T(8,128)(4,1)} %iota_compare_fusion) | copy-start | bytes 49156
  191.4 5.8 %collective-permute-start.8 = (bf16[128,128]{0,1:T(8,128)(2,1)S(1)}, bf16[128,128]{0,1:T(8,128)(2,1)S(1)}, u32[]{:S(2)}, u32[]{:S(2)}) collective-permute-start(bf16[128,128]{0,1:T(8,128)(2,1)S(1)} %maximum_select_fusion.5), channel_id=1, source_target_pairs={{0,2},{1,3},{2,0},{3,1},{4,6},{5,7},{6,4},{7,5},{8,10},{9,11},{10,... | collective-permute-start | bytes 98312 | tf_op jit(solution)/shard_map/ppermute | solution.py:18
  (3 other events, 8.5 us)
Sparse Core Ops, SparseCore 0:
  10.8 43.0 all-gather.2
  69.5 69.4 reduce-scatter.2
  150.0 34.9 all-gather.4
  200.6 69.8 reduce-scatter.4
where the time goes:
time: 280 us; the launch traced here: 279 us
  waiting for transfers between devices  197 us (70%)
  starting transfers between devices  31.5 us (11%)
  between operations  16.2 us (6%)
  other arithmetic  14.7 us (5%)
  matrix products  14.3 us (5%)
  local copies, waits for them, and re-layouts  4.74 us (2%)
    reduce_scatter x2, waiting for transfers between devices, shards(): lax.psum_scatter(jnp.dot(attended, weight_out, preferred_element_type=jnp...  129 us
    all_gather x2, waiting for transfers between devices, shards(): block_rows = lax.all_gather(normed, 'tp', axis=0, tiled=True)  49 us
    ppermute x6, starting transfers between devices, from_partner(): lax.ppermute(array, axis, [(i, i ^ 1 << stride) for i in range(lax.axis_s...  16.1 us
    ppermute x3, starting transfers between devices, shifted(): return lax.ppermute(block, axis, route)  15.2 us
    ppermute x6, waiting for transfers between devices, from_partner(): lax.ppermute(array, axis, [(i, i ^ 1 << stride) for i in range(lax.axis_s...  9.69 us
    ppermute x3, waiting for transfers between devices, shifted(): return lax.ppermute(block, axis, route)  8.9 us
  transfers between devices with their start and end apart: 13, of which 9 were waited for; matrix products, arithmetic and copies ran while one was open for 6% of the time, Pallas kernels for 0%

commit v1 on v0

v1 whole, which is shorter than its diff:
```python
import jax
import jax.numpy as jnp
import numpy as np
from jax import lax
from jax.experimental import pallas as pl
from jax.experimental.pallas import tpu as pltpu
from jax.sharding import PartitionSpec as P

KV_HEADS = 4
HD = 128
SPAN = 128
PREFIX = 1536
SPANS = 64
norm_eps = 1e-05
rope_base = 500000.0
MIB = 1 << 20


def rope_tables():
    inverse = rope_base ** (-np.arange(0, HD, 2, dtype=np.float64) / HD)
    inverse = np.concatenate([inverse, inverse])
    chips, ticks, tokens = SPAN // 16, 2, 8
    place = np.arange(chips)[None, :, None, None] * 2 + np.arange(2)[:, None, None, None]
    token = place * tokens + np.arange(tokens)[None, None, None, :]
    token = np.broadcast_to(token, (2, chips, ticks, tokens)).reshape(2, SPAN, 1)
    start = np.arange(SPANS)[:, None] * SPAN
    return [
        np.asarray(f(p * inverse), np.float32) for p in (token, start) for f in (np.cos, np.sin)
    ]


def norm_kernel(residual_ref, earlier_ref, gain_ref, out_ref):
    gain = gain_ref[...].astype(jnp.float32)
    rows = jnp.concatenate(
        [residual_ref[...].astype(jnp.float32), earlier_ref[...].astype(jnp.float32)], axis=0
    )
    mean_square = jnp.mean(rows * rows, axis=-1, keepdims=True)
    normed = (rows * lax.rsqrt(mean_square + norm_eps) * gain).astype(jnp.bfloat16)
    for copy in range(out_ref.shape[0]):
        out_ref[copy] = normed


def project_kernel(
    info_ref, own_ref, other_ref, wq_ref, wkv_ref, cos_tok, sin_tok, cos_span, sin_span,
    q_ref, kv_ref, q_acc, kv_acc,
):
    step = pl.program_id(0)

    @pl.when(step == 0)
    def _():
        q_acc[...] = jnp.zeros_like(q_acc)
        kv_acc[...] = jnp.zeros_like(kv_acc)

    rows = jnp.concatenate([own_ref[...], other_ref[...]], axis=0)
    q_acc[...] += jnp.dot(rows, wq_ref[...], preferred_element_type=jnp.float32)
    kv_acc[...] += lax.dot_general(
        rows, wkv_ref[...], (((1,), (1,)), ((), ())), preferred_element_type=jnp.float32
    )

    @pl.when(step == pl.num_programs(0) - 1)
    def _():
        core, z_place = info_ref[3], info_ref[4]
        row = lax.broadcasted_iota(jnp.int32, (SPAN, HD), 0)
        lane = lax.broadcasted_iota(jnp.int32, (SPAN, HD), 1)
        early = (row // 8) % 2 == 0
        cos_a = jnp.where(early, cos_span[pl.ds(info_ref[0], 1), :], cos_span[pl.ds(info_ref[1], 1), :])
        sin_a = jnp.where(early, sin_span[pl.ds(info_ref[0], 1), :], sin_span[pl.ds(info_ref[1], 1), :])
        for half in range(2):
            side = core if half == 0 else 1 - core
            cos_b, sin_b = cos_tok[side], sin_tok[side]
            cosine = cos_b * cos_a - sin_b * sin_a
            sine = sin_b * cos_a + cos_b * sin_a
            sine = jnp.where(lane < HD // 2, -sine, sine)
            here = pl.ds(half * SPAN, SPAN)

            def rotated(values):
                return (values * cosine + pltpu.roll(values, HD // 2, 1) * sine).astype(jnp.bfloat16)

            for head in range(q_ref.shape[1] // HD):
                columns = pl.ds(head * HD, HD)
                q_ref[here, columns] = rotated(q_acc[here, columns])
            pairs = kv_acc[here, :].astype(jnp.bfloat16)
            keys = rotated(pairs.astype(jnp.float32))
            kv_ref[here, :] = jnp.where(z_place == 0, keys, pairs)


def attend_kernel(info_ref, q_ref, kv_own_ref, kv_other_ref, cache_ref, wout_ref, att_ref, part_ref):
    length, core, z_place = info_ref[2], info_ref[3], info_ref[4]
    kv_own, kv_other = kv_own_ref[...], kv_other_ref[...]
    new_keys = jnp.where(z_place == 0, kv_own, kv_other)
    new_values = jnp.where(z_place == 0, kv_other, kv_own)
    rows = 2 * SPAN

    def place(index):
        half = index // SPAN
        side = jnp.where(half == 0, core, 1 - core)
        token = (((index // 16) % 8) * 2 + side) * 8 + index % 8
        return (index // 8) % 2, token

    row_tick, row_token = place(lax.broadcasted_iota(jnp.int32, (rows, 1), 0))
    key_tick, key_token = place(lax.broadcasted_iota(jnp.int32, (1, rows), 1))
    fresh = (row_tick == key_tick) & (key_token <= row_token)
    slots = lax.broadcasted_iota(jnp.int32, (1, PREFIX), 1)
    cached = slots < length
    contract = (((1,), (1,)), ((), ()))
    for head in range(q_ref.shape[1] // HD):
        columns = pl.ds(head * HD, HD)
        queries = q_ref[:, columns]
        s_prefix = lax.dot_general(
            queries, cache_ref[:, pl.ds(0, HD)], contract, preferred_element_type=jnp.float32
        )
        s_fresh = lax.dot_general(queries, new_keys, contract, preferred_element_type=jnp.float32)
        scale = HD ** (-0.5)
        s_prefix = jnp.where(cached, s_prefix * scale, -jnp.inf)
        s_fresh = jnp.where(fresh, s_fresh * scale, -jnp.inf)
        peak = jnp.maximum(
            jnp.max(s_prefix, axis=-1, keepdims=True), jnp.max(s_fresh, axis=-1, keepdims=True)
        )
        e_prefix = jnp.exp(s_prefix - peak)
        e_fresh = jnp.exp(s_fresh - peak)
        total = jnp.sum(e_prefix, axis=-1, keepdims=True) + jnp.sum(e_fresh, axis=-1, keepdims=True)
        summed = jnp.dot(
            e_prefix.astype(jnp.bfloat16), cache_ref[:, pl.ds(HD, HD)], preferred_element_type=jnp.float32
        ) + jnp.dot(e_fresh.astype(jnp.bfloat16), new_values, preferred_element_type=jnp.float32)
        att_ref[:, columns] = (summed / total).astype(jnp.bfloat16)
    part_ref[...] = jnp.dot(
        att_ref[pl.ds(SPAN, SPAN), :], wout_ref[...], preferred_element_type=jnp.float32
    ).astype(jnp.bfloat16)


def out_kernel(att_ref, wout_ref, part_ref):
    part_ref[...] = jnp.dot(att_ref[...], wout_ref[...], preferred_element_type=jnp.float32)


def swapped(array, bit):
    return lax.ppermute(array, "tp", [(i, i ^ bit) for i in range(lax.axis_size("tp"))])


def to_next_section(array):
    sections = lax.axis_size("segment")
    return lax.ppermute(array, "segment", [(i, i + 1) for i in range(sections - 1)])


def shards(
    residual, pending, span_index, prefix_len, norm_gain, w_query, w_kv, w_out, prefix_cache
):
    tp_size = lax.axis_size("tp")
    tp_place = lax.axis_index("tp")
    core, z_place = tp_place % 2, tp_place // 2 % 2
    width = residual.shape[2]
    tokens = residual.shape[1]
    chips = tp_size // 2
    same_core = [list(range(c, tp_size, 2)) for c in range(2)]
    same_chip = [[i, i + 1] for i in range(0, tp_size, 2)]
    same_head = [list(range(i, i + 4)) for i in range(0, tp_size, 4)]
    vmem = pl.BlockSpec(memory_space=pltpu.VMEM)
    smem = pl.BlockSpec(memory_space=pltpu.SMEM)

    cache = lax.all_gather(prefix_cache[0], "tp", axis=0, tiled=True, axis_index_groups=same_head)
    pair_weight = lax.all_gather(
        jnp.transpose(w_kv[0]), "tp", axis=0, tiled=True, axis_index_groups=same_chip
    )

    carried = (residual[0].astype(jnp.float32) + pending[0].astype(jnp.float32)).astype(jnp.bfloat16)
    index_lanes = jnp.broadcast_to(span_index.astype(jnp.bfloat16)[:, None], (tokens, HD))
    earlier = to_next_section(jnp.concatenate([carried, index_lanes], axis=1))
    earlier_index = earlier[0, width].astype(jnp.int32)
    earlier = earlier[:, :width]
    info = jnp.stack([span_index[0], earlier_index, prefix_len[0], core, z_place])

    normed = pl.pallas_call(
        norm_kernel,
        out_shape=jax.ShapeDtypeStruct((chips, 2 * tokens, width), jnp.bfloat16),
        in_specs=[vmem, vmem, vmem],
        out_specs=vmem,
        compiler_params=pltpu.CompilerParams(vmem_limit_bytes=16 * MIB),
    )(residual[0], earlier, norm_gain)
    own = lax.all_to_all(normed, "tp", 0, 0, axis_index_groups=same_core)
    own = own.reshape(SPAN, width)
    other = swapped(own, 1)

    steps = 4
    depth = width // steps
    columns = w_query.shape[2]
    tables = [jnp.asarray(t) for t in rope_tables()]
    whole = lambda a: pl.BlockSpec(a.shape, lambda k: (0,) * a.ndim)
    q, pairs = pl.pallas_call(
        project_kernel,
        grid=(steps,),
        out_shape=[
            jax.ShapeDtypeStruct((2 * SPAN, columns), jnp.bfloat16),
            jax.ShapeDtypeStruct((2 * SPAN, HD), jnp.bfloat16),
        ],
        in_specs=[
            smem,
            pl.BlockSpec((SPAN, depth), lambda k: (0, k)),
            pl.BlockSpec((SPAN, depth), lambda k: (0, k)),
            pl.BlockSpec((depth, columns), lambda k: (k, 0)),
            pl.BlockSpec((HD, depth), lambda k: (0, k)),
        ]
        + [whole(t) for t in tables],
        out_specs=[
            pl.BlockSpec((2 * SPAN, columns), lambda k: (0, 0)),
            pl.BlockSpec((2 * SPAN, HD), lambda k: (0, 0)),
        ],
        scratch_shapes=[
            pltpu.VMEM((2 * SPAN, columns), jnp.float32),
            pltpu.VMEM((2 * SPAN, HD), jnp.float32),
        ],
        compiler_params=pltpu.CompilerParams(vmem_limit_bytes=24 * MIB),
    )(info, own, other, w_query[0], pair_weight, *tables)
    other_pairs = swapped(pairs, 2)

    attended, part_other = pl.pallas_call(
        attend_kernel,
        out_shape=[
            jax.ShapeDtypeStruct((2 * SPAN, columns), jnp.bfloat16),
            jax.ShapeDtypeStruct((SPAN, width), jnp.bfloat16),
        ],
        in_specs=[smem, vmem, vmem, vmem, vmem, vmem],
        out_specs=[vmem, vmem],
        compiler_params=pltpu.CompilerParams(vmem_limit_bytes=32 * MIB),
    )(info, q, pairs, other_pairs, cache, w_out[0])
    arrived = swapped(part_other, 1)
    part_own = pl.pallas_call(
        out_kernel,
        out_shape=jax.ShapeDtypeStruct((SPAN, width), jnp.float32),
        in_specs=[vmem, vmem],
        out_specs=vmem,
        compiler_params=pltpu.CompilerParams(vmem_limit_bytes=24 * MIB),
        cost_estimate=pl.CostEstimate(
            flops=2 * SPAN * columns * width, bytes_accessed=8 * MIB, transcendentals=0
        ),
    )(attended[:SPAN], w_out[0])
    chip_part = (part_own + arrived.astype(jnp.float32)).astype(jnp.bfloat16)
    parts = lax.all_to_all(
        chip_part.reshape(chips, 2 * tokens, width), "tp", 0, 0, axis_index_groups=same_core
    )
    summed = jnp.sum(parts.astype(jnp.float32), axis=0).astype(jnp.bfloat16)
    late_output = to_next_section(summed[:tokens])
    final_carried = (earlier.astype(jnp.float32) + late_output.astype(jnp.float32)).astype(jnp.bfloat16)
    return (final_carried[None], summed[tokens:][None])


def solution(mesh):
    in_specs = (
        P("segment", "tp", None),
        P("segment", "tp", None),
        P("segment"),
        P("segment"),
        P("segment", None),
        P("segment", None, "tp"),
        P("segment", None, "tp"),
        P("segment", "tp", None),
        P("segment", "tp", None),
    )
    out_specs = (P("segment", "tp", None), P("segment", "tp", None))
    return jax.shard_map(shards, mesh=mesh, in_specs=in_specs, out_specs=out_specs, check_vma=False)
```

time: 280 us -> 116 us (0.41)
  the two profiles are of different devices: /device:TPU:24 before, /device:TPU:32 now
where the time goes in v1:
time: 116 us; the launch traced here: 115 us
  waiting for transfers between devices  32.2 us (28%)
  blocking collectives  29.1 us (25%)
  starting transfers between devices  23.7 us (20%)
  between operations  16.2 us (14%)
  Pallas kernels  8.22 us (7%)
  local copies, waits for them, and re-layouts  4.07 us (4%)
  other arithmetic  1.94 us (2%)
    all_to_all x1, blocking collectives, shards(): lax.all_to_all(chip_part.reshape(chips, 2 * tokens, width), 'tp', 0, 0, a...  20.7 us
    ppermute x2, waiting for transfers between devices, to_next_section(): lax.ppermute(array, 'segment', [(i, i + 1) for i in range(sections - 1)])  14.3 us
    all_to_all x1, waiting for transfers between devices, shards(): own = lax.all_to_all(normed, 'tp', 0, 0, axis_index_groups=same_core)  13.6 us
    ppermute x2, starting transfers between devices, to_next_section(): lax.ppermute(array, 'segment', [(i, i + 1) for i in range(sections - 1)])  10.9 us
    all_gather x1, blocking collectives, shards(): lax.all_gather(prefix_cache[0], 'tp', axis=0, tiled=True, axis_index_grou...  8.39 us
    ppermute x3, starting transfers between devices, swapped(): lax.ppermute(array, 'tp', [(i, i ^ bit) for i in range(lax.axis_size('tp'...  7.72 us
    all_to_all x1, starting transfers between devices, shards(): own = lax.all_to_all(normed, 'tp', 0, 0, axis_index_groups=same_core)  5.11 us
    pallas_call x1, Pallas kernels, shards(): pl.pallas_call(project_kernel, grid=(steps,), out_shape=[jax.ShapeDtypeSt...  3.74 us
  transfers between devices with their start and end apart: 7, of which 5 were waited for; matrix products, arithmetic and copies ran while one was open for 1% of the time, Pallas kernels for 0%

profile of v1, /device:TPU:32, one launch (start us, length us, event | category | flops | bytes accessed | tf_op | source)
XLA Modules:
  0.0 115.4 jit_solution(13850573203388105530)
XLA Ops:
  7.9 0.9 fusion
  8.8 6.2 %collective-permute-start = (bf16[8,4224]{1,0:T(8,128)(2,1)S(1)}, bf16[8,4224]{1,0:T(8,128)(2,1)S(1)}, u32[]{:S(2)}, u32[]{:S(2)}) collective-permute-start(bf16[8,4224]{1,0:T(8,128)(2,1)S(1)} %concatenate.3), channel_id=1, source_target_pairs={{0,16},{16,32},{32,48},{48,64},{64,80},{80,96},{96,112},{112,128},... | collective-permute-start | bytes 202760 | tf_op jit(solution)/shard_map/ppermute | solution.py:141
  15.1 8.3 %collective-permute-done = bf16[8,4224]{1,0:T(8,128)(2,1)S(1)} collective-permute-done((bf16[8,4224]{1,0:T(8,128)(2,1)S(1)}, bf16[8,4224]{1,0:T(8,128)(2,1)S(1)}, u32[]{:S(2)}, u32[]{:S(2)}) %collective-permute-start) | collective-permute-done | bytes 67616 | tf_op jit(solution)/shard_map/ppermute | solution.py:141
  23.4 0.8 copy-done.3
  24.2 0.7 copy-done.8
  24.9 1.2 %shard_map.140 = bf16[8,16,4096]{2,1,0:T(8,128)(2,1)} custom-call(bf16[8,4096]{1,0:T(8,128)(2,1)S(1)} %bitcast.28, bf16[8,4096]{1,0:T(8,128)(2,1)S(1)} %slice.20.earlier_ref, bf16[1,4096]{1,0:T(2,128)(2,1)S(1)} %copy-done.8), custom_call_target="tpu_custom_call" | custom-call | tf_op jit(solution)/shard_map/pallas_call | solution.py:171
  26.1 5.1 %all-to-all-start = ((bf16[8,16,4096]{2,1,0:T(8,128)(2,1)}), bf16[8,16,4096]{2,1,0:T(8,128)(2,1)S(1)}, u32[]{:S(2)}, u32[]{:S(2)}) async-start(bf16[8,16,4096]{2,1,0:T(8,128)(2,1)} %shard_map.140), calls=%async_computation | async-start | bytes 2097152 | tf_op jit(solution)/shard_map/all_to_all | solution.py:178
  31.3 0.7 all-gather.3.cloned.1.call-update
  31.9 13.6 %all-to-all-done = bf16[8,16,4096]{2,1,0:T(8,128)(2,1)S(1)} async-done(((bf16[8,16,4096]{2,1,0:T(8,128)(2,1)}), bf16[8,16,4096]{2,1,0:T(8,128)(2,1)S(1)}, u32[]{:S(2)}, u32[]{:S(2)}) %all-to-all-start) | async-done | bytes 1048608 | tf_op jit(solution)/shard_map/all_to_all | solution.py:178
  45.6 1.9 %collective-permute-start.1 = (bf16[128,4096]{1,0:T(8,128)(2,1)S(1)}, bf16[128,4096]{1,0:T(8,128)(2,1)}, u32[]{:S(2)}, u32[]{:S(2)}) collective-permute-start(bf16[128,4096]{1,0:T(8,128)(2,1)S(1)} %bitcast.24), channel_id=1, source_target_pairs={{0,1},{1,0},{2,3},{3,2},{4,5},{5,4},{6,7},{7,6},{8,9},{9,8},{10,11... | collective-permute-start | bytes 3145736 | tf_op jit(solution)/shard_map/ppermute | solution.py:136
  48.2 0.5 slice.21
  49.5 1.7 %all-gather.3.cloned.1.call-done.wkv_ref = bf16[128,4096]{1,0:T(8,128)(2,1)} async-done(((bf16[64,4096]{1,0:T(8,128)(2,1)}), bf16[128,4096]{1,0:T(8,128)(2,1)}) %all-gather.3.cloned.1.call-update) | async-done | bytes 1048592 | tf_op jit(solution)/shard_map/all_gather | solution.py:160
  51.2 1.2 %copy-done.2 = bf16[128,4096]{1,0:T(8,128)(2,1)S(1)} copy-done((bf16[128,4096]{1,0:T(8,128)(2,1)S(1)}, bf16[128,4096]{1,0:T(8,128)(2,1)}, u32[]{:S(2)}) %copy-start.2) | copy-done | bytes 1048600
  52.4 3.7 %shard_map.141 = (bf16[256,256]{1,0:T(8,128)(2,1)S(1)}, bf16[256,128]{1,0:T(8,128)(2,1)S(1)}) custom-call(s32[5]{0:T(128)S(1)} %stack.19.info_ref, bf16[128,4096]{1,0:T(8,128)(2,1)S(1)} %bitcast.25, bf16[128,4096]{1,0:T(8,128)(2,1)} %collective-permute-done.1.other_ref, bf16[4096,256]{1,0:T(8,128)(2,1)S(1)} %bitcast.27, bf16[128,4096]{1,0:T(8,128)(2,1)S(1)} %copy-done.2, ...), custom_call_target="tpu_custom_call" | custom-call | tf_op jit(solution)/shard_map/pallas_call | solution.py:187
  56.1 3.6 %collective-permute-start.2 = (bf16[256,128]{1,0:T(8,128)(2,1)S(1)}, bf16[256,128]{1,0:T(8,128)(2,1)S(1)}, u32[]{:S(2)}, u32[]{:S(2)}) collective-permute-start(bf16[256,128]{1,0:T(8,128)(2,1)S(1)} %get-tuple-element.7.kv_own_ref), channel_id=1, source_target_pairs={{0,2},{1,3},{2,0},{3,1},{4,6},{5,7},{6,4},{7,5},{8,10},{9,11},{10,... | collective-permute-start | bytes 196616 | tf_op jit(solution)/shard_map/ppermute | solution.py:136
  59.7 8.4 %all-gather = bf16[1,1536,256]{2,1,0:T(8,128)(2,1)S(1)} all-gather(bf16[1,384,256]{2,1,0:T(8,128)(2,1)S(1)} %copy-done.9), channel_id=2, replica_groups={{0,1,2,3},{4,5,6,7},{8,9,10,11},{12,13,14,15},{16,17,18,19},{20,21,22,2..., dimensions={1}, use_global_device_ids=true | all-gather | bytes 983040 | tf_op jit(solution)/shard_map/all_gather | solution.py:159
  68.1 2.8 %shard_map.142 = (bf16[256,256]{1,0:T(8,128)(2,1)S(1)}, bf16[128,4096]{1,0:T(8,128)(2,1)S(1)}) custom-call(s32[5]{0:T(128)S(1)} %stack.19.info_ref, bf16[256,256]{1,0:T(8,128)(2,1)S(1)} %get-tuple-element.6.q_ref, bf16[256,128]{1,0:T(8,128)(2,1)S(1)} %get-tuple-element.7.kv_own_ref, bf16[256,128]{1,0:T(8,128)(2,1)S(1)} %collective-permute-done.2.kv_other_ref, ...), custom_call_target="tpu_custom_call" | custom-call | tf_op jit(solution)/shard_map/pallas_call | solution.py:214
  71.0 2.3 %collective-permute-start.3 = (bf16[128,4096]{1,0:T(8,128)(2,1)S(1)}, bf16[128,4096]{1,0:T(8,128)(2,1)S(1)}, u32[]{:S(2)}, u32[]{:S(2)}) collective-permute-start(bf16[128,4096]{1,0:T(8,128)(2,1)S(1)} %get-tuple-element.9), channel_id=1, source_target_pairs={{0,1},{1,0},{2,3},{3,2},{4,5},{5,4},{6,7},{7,6},{8,9},{9,8},{10,11... | collective-permute-start | bytes 3145736 | tf_op jit(solution)/shard_map/ppermute | solution.py:136
  73.7 1.8 %collective-permute-done.3 = bf16[128,4096]{1,0:T(8,128)(2,1)S(1)} collective-permute-done((bf16[128,4096]{1,0:T(8,128)(2,1)S(1)}, bf16[128,4096]{1,0:T(8,128)(2,1)S(1)}, u32[]{:S(2)}, u32[]{:S(2)}) %collective-permute-start.3) | collective-permute-done | bytes 1048608 | tf_op jit(solution)/shard_map/ppermute | solution.py:136
  75.7 20.7 %all_to_all.10 = bf16[8,16,4096]{2,1,0:T(8,128)(2,1)S(1)} all-to-all(bf16[8,16,4096]{2,1,0:T(8,128)(2,1)S(1)} %bitcast.29), channel_id=1, replica_groups={{0,2,4,6,8,10,12,14},{1,3,5,7,9,11,13,15},{16,18,20,22,24,26,28,30},{17..., dimensions={0} | all-to-all | bytes 2097152 | tf_op jit(solution)/shard_map/all_to_all | solution.py:236
  96.5 0.6 slice_bitcast_fusion
  97.2 4.6 %collective-permute-start.4 = (bf16[8,4096]{1,0:T(8,128)(2,1)S(1)}, bf16[8,4096]{1,0:T(8,128)(2,1)S(1)}, u32[]{:S(2)}, u32[]{:S(2)}) collective-permute-start(bf16[8,4096]{1,0:T(8,128)(2,1)S(1)} %get-tuple-element.11), channel_id=1, source_target_pairs={{0,16},{16,32},{32,48},{48,64},{64,80},{80,96},{96,112},{112,128},... | collective-permute-start | bytes 196616 | tf_op jit(solution)/shard_map/ppermute | solution.py:141
  101.8 6.0 %collective-permute-done.4 = bf16[8,4096]{1,0:T(8,128)(2,1)S(1)} collective-permute-done((bf16[8,4096]{1,0:T(8,128)(2,1)S(1)}, bf16[8,4096]{1,0:T(8,128)(2,1)S(1)}, u32[]{:S(2)}, u32[]{:S(2)}) %collective-permute-start.4) | collective-permute-done | bytes 65568 | tf_op jit(solution)/shard_map/ppermute | solution.py:141
  107.9 0.6 fusion.1
  (27 shorter events, 1.0 us)
Async XLA Ops:
  7.8 43.3 %copy-start.4 = (f32[2,128,128]{2,1,0:T(8,128)S(1)}, f32[2,128,128]{2,1,0:T(8,128)}, u32[]{:S(2)}) copy-start(f32[2,128,128]{2,1,0:T(8,128)} %constant.44.clone.sin_tok) | copy-start | bytes 393220
  7.8 43.3 %copy-start.6 = (f32[64,128]{1,0:T(8,128)S(1)}, f32[64,128]{1,0:T(8,128)}, u32[]{:S(2)}) copy-start(f32[64,128]{1,0:T(8,128)} %constant.46.clone.sin_span) | copy-start | bytes 98308
  7.8 43.3 %copy-start.7 = (f32[64,128]{1,0:T(8,128)S(1)}, f32[64,128]{1,0:T(8,128)}, u32[]{:S(2)}) copy-start(f32[64,128]{1,0:T(8,128)} %constant.45.clone.cos_span) | copy-start | bytes 98308
  8.8 42.3 %copy-start.1 = (bf16[1,4096,256]{2,1,0:T(8,128)(2,1)S(1)}, bf16[1,4096,256]{2,1,0:T(8,128)(2,1)}, u32[]{:S(2)}) copy-start(bf16[1,4096,256]{2,1,0:T(8,128)(2,1)} %param.18) | copy-start | bytes 6291460
  8.8 14.5 %collective-permute-start = (bf16[8,4224]{1,0:T(8,128)(2,1)S(1)}, bf16[8,4224]{1,0:T(8,128)(2,1)S(1)}, u32[]{:S(2)}, u32[]{:S(2)}) collective-permute-start(bf16[8,4224]{1,0:T(8,128)(2,1)S(1)} %concatenate.3), channel_id=1, source_target_pairs={{0,16},{16,32},{32,48},{48,64},{64,80},{80,96},{96,112},{112,128},... | collective-permute-start | bytes 202760 | tf_op jit(solution)/shard_map/ppermute | solution.py:141
  23.4 0.8 copy-start.3
  24.2 0.7 copy-start.8
  24.9 26.2 %copy-start.5 = (f32[2,128,128]{2,1,0:T(8,128)S(1)}, f32[2,128,128]{2,1,0:T(8,128)}, u32[]{:S(2)}) copy-start(f32[2,128,128]{2,1,0:T(8,128)} %constant.43.clone.cos_tok) | copy-start | bytes 393220
  26.1 19.5 %all-to-all-start = ((bf16[8,16,4096]{2,1,0:T(8,128)(2,1)}), bf16[8,16,4096]{2,1,0:T(8,128)(2,1)S(1)}, u32[]{:S(2)}, u32[]{:S(2)}) async-start(bf16[8,16,4096]{2,1,0:T(8,128)(2,1)} %shard_map.140), calls=%async_computation | async-start | bytes 2097152 | tf_op jit(solution)/shard_map/all_to_all | solution.py:178
  31.2 19.9 %all-gather.3.cloned.1.call-start = ((), (), s32[]{:S(2)}) async-start(), calls=%async_computation.2 | async-start | bytes 1572864 | tf_op jit(solution)/shard_map/all_gather | solution.py:160
  45.6 5.5 %collective-permute-start.1 = (bf16[128,4096]{1,0:T(8,128)(2,1)S(1)}, bf16[128,4096]{1,0:T(8,128)(2,1)}, u32[]{:S(2)}, u32[]{:S(2)}) collective-permute-start(bf16[128,4096]{1,0:T(8,128)(2,1)S(1)} %bitcast.24), channel_id=1, source_target_pairs={{0,1},{1,0},{2,3},{3,2},{4,5},{5,4},{6,7},{7,6},{8,9},{9,8},{10,11... | collective-permute-start | bytes 3145736 | tf_op jit(solution)/shard_map/ppermute | solution.py:136
  51.2 1.2 %copy-start.2 = (bf16[128,4096]{1,0:T(8,128)(2,1)S(1)}, bf16[128,4096]{1,0:T(8,128)(2,1)}, u32[]{:S(2)}) copy-start(bf16[128,4096]{1,0:T(8,128)(2,1)} %all-gather.3.cloned.1.call-done.wkv_ref) | copy-start | bytes 3145732
  52.4 7.3 %copy-start.9 = (bf16[1,384,256]{2,1,0:T(8,128)(2,1)S(1)}, bf16[1,384,256]{2,1,0:T(8,128)(2,1)}, u32[]{:S(2)}) copy-start(bf16[1,384,256]{2,1,0:T(8,128)(2,1)} %param.21) | copy-start | bytes 589828
  52.4 15.7 %copy-start = (bf16[1,256,4096]{2,1,0:T(8,128)(2,1)S(1)}, bf16[1,256,4096]{2,1,0:T(8,128)(2,1)}, u32[]{:S(2)}) copy-start(bf16[1,256,4096]{2,1,0:T(8,128)(2,1)} %param.20) | copy-start | bytes 6291460
  56.1 12.0 %collective-permute-start.2 = (bf16[256,128]{1,0:T(8,128)(2,1)S(1)}, bf16[256,128]{1,0:T(8,128)(2,1)S(1)}, u32[]{:S(2)}, u32[]{:S(2)}) collective-permute-start(bf16[256,128]{1,0:T(8,128)(2,1)S(1)} %get-tuple-element.7.kv_own_ref), channel_id=1, source_target_pairs={{0,2},{1,3},{2,0},{3,1},{4,6},{5,7},{6,4},{7,5},{8,10},{9,11},{10,... | collective-permute-start | bytes 196616 | tf_op jit(solution)/shard_map/ppermute | solution.py:136
  71.0 4.6 %collective-permute-start.3 = (bf16[128,4096]{1,0:T(8,128)(2,1)S(1)}, bf16[128,4096]{1,0:T(8,128)(2,1)S(1)}, u32[]{:S(2)}, u32[]{:S(2)}) collective-permute-start(bf16[128,4096]{1,0:T(8,128)(2,1)S(1)} %get-tuple-element.9), channel_id=1, source_target_pairs={{0,1},{1,0},{2,3},{3,2},{4,5},{5,4},{6,7},{7,6},{8,9},{9,8},{10,11... | collective-permute-start | bytes 3145736 | tf_op jit(solution)/shard_map/ppermute | solution.py:136
  97.2 10.7 %collective-permute-start.4 = (bf16[8,4096]{1,0:T(8,128)(2,1)S(1)}, bf16[8,4096]{1,0:T(8,128)(2,1)S(1)}, u32[]{:S(2)}, u32[]{:S(2)}) collective-permute-start(bf16[8,4096]{1,0:T(8,128)(2,1)S(1)} %get-tuple-element.11), channel_id=1, source_target_pairs={{0,16},{16,32},{32,48},{48,64},{64,80},{80,96},{96,112},{112,128},... | collective-permute-start | bytes 196616 | tf_op jit(solution)/shard_map/ppermute | solution.py:141
Sparse Core Ops, SparseCore 0:
  34.1 16.9 all-gather.2

commit v2 on v0

v2 whole, which is shorter than its diff:
```python
import functools

import jax
import jax.numpy as jnp
import numpy as np
from jax import lax
from jax.experimental import pallas as pl
from jax.experimental.pallas import tpu as pltpu
from jax.sharding import PartitionSpec as P

KV_HEADS = 4
HD = 128
SPAN = 128
PREFIX = 1536
SPANS = 64
norm_eps = 1e-05
rope_base = 500000.0
MIB = 1 << 20


contract_last = (((1,), (1,)), ((), ()))


def rope_tables():
    inverse = rope_base ** (-np.arange(0, HD, 2, dtype=np.float64) / HD)
    inverse = np.concatenate([inverse, inverse])
    chips, tokens = SPAN // 16, 8
    place = np.arange(chips)[None, :, None] * 2 + np.arange(2)[:, None, None]
    token = (place * tokens + np.arange(tokens)[None, None, :]).reshape(2, SPAN // 2, 1)
    start = np.arange(SPANS)[:, None] * SPAN
    return [
        np.asarray(f(p * inverse), np.float32) for p in (token, start) for f in (np.cos, np.sin)
    ]


def carry_kernel(span_ref, residual_ref, pending_ref, out_ref):
    tokens, width = residual_ref.shape
    carried = residual_ref[...].astype(jnp.float32) + pending_ref[...].astype(jnp.float32)
    out_ref[:, :width] = carried.astype(jnp.bfloat16)
    index = jnp.full((tokens, out_ref.shape[1] - width), span_ref[0], jnp.int32)
    out_ref[:, width:] = index.astype(jnp.float32).astype(jnp.bfloat16)


def normalised(rows_ref, gain_ref):
    rows = rows_ref[:, : gain_ref.shape[1]].astype(jnp.float32)
    mean_square = jnp.mean(rows * rows, axis=-1, keepdims=True)
    return rows * lax.rsqrt(mean_square + norm_eps) * gain_ref[...].astype(jnp.float32)


def norm_kernel(residual_ref, earlier_ref, gain_ref, out_ref):
    ticks = [normalised(ref, gain_ref) for ref in (residual_ref, earlier_ref)]
    normed = jnp.concatenate(ticks, axis=0).astype(jnp.bfloat16)
    for copy in range(out_ref.shape[0]):
        out_ref[copy] = normed


def table_kernel(span_ref, info_ref, earlier_ref, cos_tok, sin_tok, cos_span, sin_span, out_ref):
    core = info_ref[0]
    late = earlier_ref[:, -HD:].astype(jnp.float32)[:1].astype(jnp.int32)
    spans = lax.broadcasted_iota(jnp.int32, cos_span.shape, 0)
    low = lax.broadcasted_iota(jnp.int32, out_ref.shape[2:], 1) < HD // 2
    cos_b, sin_b = cos_tok[core], sin_tok[core]
    for tick, index in enumerate((span_ref[0], late)):
        cos_a, sin_a = [
            jnp.sum(jnp.where(spans == index, table[...], 0.0), axis=0, keepdims=True)
            for table in (cos_span, sin_span)
        ]
        sine = sin_b * cos_a + cos_b * sin_a
        out_ref[0, tick] = cos_b * cos_a - sin_b * sin_a
        out_ref[1, tick] = jnp.where(low, -sine, sine)


def of_tick(values, tick):
    rows = values.shape[0] // 2
    return values.reshape(rows // 8, 2, 8, HD)[:, tick].reshape(rows, HD)


def rotated(values, table_ref, tick):
    turned = pltpu.roll(values, HD // 2, 1) * table_ref[1, tick]
    return (values * table_ref[0, tick] + turned).astype(jnp.bfloat16)


def query_kernel(rows_ref, weight_ref, table_ref, q_ref):
    queries = jnp.dot(rows_ref[...], weight_ref[...], preferred_element_type=jnp.float32)
    rows = rows_ref.shape[0] // 2
    for tick in range(2):
        for head in range(queries.shape[1] // HD):
            values = of_tick(queries[:, head * HD : (head + 1) * HD], tick)
            q_ref[tick, pl.ds(head * rows, rows), :] = rotated(values, table_ref, tick)


def pair_kernel(info_ref, rows_ref, own_ref, other_ref, table_ref, kv_ref):
    core, z_place = info_ref[0], info_ref[1]
    weight = jnp.concatenate([own_ref[...], other_ref[...]], axis=0)
    pairs = lax.dot_general(
        rows_ref[...], weight, contract_last, preferred_element_type=jnp.float32
    )
    pairs = jnp.where(core == 0, pairs, pltpu.roll(pairs, HD // 2, 1))
    for tick in range(2):
        both = of_tick(pairs, tick).astype(jnp.bfloat16)
        keys = rotated(both.astype(jnp.float32), table_ref, tick)
        for copy in range(kv_ref.shape[0]):
            kv_ref[copy, tick] = jnp.where(z_place == 0, keys, both)


def attend_kernel(
    length_ref, info_ref, q_own, q_other, kv_ref, own, from_z, from_core, from_both,
    wout_own_any, wout_other_any, out_ref, wout_ref, sems,
):
    weight_copies = [
        pltpu.make_async_copy(source, wout_ref.at[side], sems.at[side])
        for side, source in enumerate((wout_own_any, wout_other_any))
    ]
    for copy in weight_copies:
        copy.start()
    core, z_place = info_ref[0], info_ref[1]
    chips, tokens, width = out_ref.shape
    rows = chips * tokens
    queries = jnp.concatenate([q_own[0], q_other[0]], axis=0)

    def token(index, side):
        return ((index % rows // tokens) * 2 + side) * tokens + index % tokens

    row_token = token(lax.broadcasted_iota(jnp.int32, (queries.shape[0], 1), 0), core)
    key = lax.broadcasted_iota(jnp.int32, (1, 2 * rows), 1)
    allowed = [token(key, key // rows) <= row_token]
    keys = [jnp.concatenate([kv_ref[0, 0], kv_ref[1, 0]], axis=0)]
    values = [jnp.concatenate([kv_ref[2, 0], kv_ref[3, 0]], axis=0)]
    block = own.shape[0]
    slot = lax.broadcasted_iota(jnp.int32, (1, block), 1)
    places = [(z, c) for c in (core, 1 - core) for z in (z_place, 1 - z_place)]
    for cache_ref, (z, c) in zip((own, from_z, from_core, from_both), places):
        keys.append(cache_ref[:, :HD])
        values.append(cache_ref[:, HD:])
        allowed.append((z * 2 + c) * block + slot < length_ref[0])

    scores = []
    for key, seen in zip(keys, allowed):
        score = lax.dot_general(queries, key, contract_last, preferred_element_type=jnp.float32)
        scores.append(jnp.where(seen, score * HD ** (-0.5), -jnp.inf))
    peak = functools.reduce(jnp.maximum, [jnp.max(s, axis=-1, keepdims=True) for s in scores])
    total, summed = 0.0, 0.0
    for score, value in zip(scores, values):
        weights = jnp.exp(score - peak)
        total += jnp.sum(weights, axis=-1, keepdims=True)
        summed += jnp.dot(weights.astype(jnp.bfloat16), value, preferred_element_type=jnp.float32)
    result = (summed / total).astype(jnp.bfloat16)
    heads = [result[at : at + rows] for at in range(0, queries.shape[0], rows)]
    half = len(heads) // 2
    sides = [jnp.concatenate(heads[:half], axis=1), jnp.concatenate(heads[half:], axis=1)]
    for copy in weight_copies:
        copy.wait()
    step = 1024
    for left in range(0, width, step):
        columns = pl.ds(left, step)
        part = sum(
            jnp.dot(sides[side], wout_ref[side, :, columns], preferred_element_type=jnp.float32)
            for side in range(2)
        )
        out_ref[:, :, columns] = part.reshape(chips, tokens, step).astype(jnp.bfloat16)


def swapped(array, bit):
    return lax.ppermute(array, "tp", [(i, i ^ bit) for i in range(lax.axis_size("tp"))])


def to_next_section(array):
    sections = lax.axis_size("segment")
    return lax.ppermute(array, "segment", [(i, i + 1) for i in range(sections - 1)])


def after(*arrays):
    return lax.optimization_barrier(arrays)


def shards(
    residual, pending, span_index, prefix_len, norm_gain, w_query, w_kv, w_out, prefix_cache
):
    tp_size = lax.axis_size("tp")
    tp_place = lax.axis_index("tp")
    info = jnp.stack([tp_place % 2, tp_place // 2 % 2])
    tokens, width = residual.shape[1:]
    chips = tp_size // 2
    rows = chips * tokens
    local = w_query.shape[2]
    heads = 2 * local // HD
    same_core = [list(range(c, tp_size, 2)) for c in range(2)]
    same_head = [list(range(i, i + 4)) for i in range(0, tp_size, 4)]
    smem = pl.BlockSpec(memory_space=pltpu.SMEM)
    hbm = pl.BlockSpec(memory_space=pl.ANY)
    bf16, f32 = jnp.bfloat16, jnp.float32
    cos_tok, sin_tok, cos_span, sin_span = [jnp.asarray(t) for t in rope_tables()]

    def block(shape, place=None):
        place = place or (0,) * len(shape)
        return pl.BlockSpec(shape, lambda step: place)

    def kernel(body, inputs, outs, limit, flops=1 << 20, specs=None, scratch=()):
        specs = specs or [smem if a.ndim == 1 else block(a.shape) for a in inputs]
        return pl.pallas_call(
            body,
            grid=(1,),
            out_shape=[jax.ShapeDtypeStruct(shape, dtype) for shape, dtype in outs],
            in_specs=specs,
            out_specs=[block(shape) for shape, _ in outs],
            scratch_shapes=scratch,
            compiler_params=pltpu.CompilerParams(vmem_limit_bytes=limit * MIB),
            cost_estimate=pl.CostEstimate(flops=flops, bytes_accessed=flops // 64, transcendentals=0),
        )(*inputs)

    (carried,) = kernel(
        carry_kernel, [span_index, residual[0], pending[0]], [((tokens, width + HD), bf16)], 60
    )
    earlier = to_next_section(carried)
    cache_z = swapped(prefix_cache[0], 2)
    (normed,) = kernel(
        norm_kernel,
        [residual[0], earlier, norm_gain],
        [((chips, 2 * tokens, width), bf16)],
        60,
        10 * 10**9,
    )
    normed, cache_z = after(normed, cache_z)
    gathered = lax.all_to_all(normed, "tp", 0, 0, axis_index_groups=same_core)
    gathered = gathered.reshape(2 * rows, width)

    _, late_earlier = after(normed, earlier)
    (table,) = kernel(
        table_kernel,
        [span_index, info, late_earlier, cos_tok, sin_tok, cos_span, sin_span],
        [((2, 2, rows, HD), f32)],
        16,
        flops=0,
    )
    _, pair_weight, own_w_query, own_w_out, cache_own, cache_z = after(
        normed, jnp.transpose(w_kv[0]), w_query[0], w_out[0], prefix_cache[0], cache_z
    )
    other_pair_weight = swapped(pair_weight, 1)
    other_w_query = swapped(own_w_query, 1)
    caches = [cache_own, cache_z, swapped(cache_own, 1), swapped(cache_z, 1)]
    other_w_out = swapped(own_w_out, 1)

    (pairs,) = kernel(
        pair_kernel,
        [info, gathered, pair_weight, other_pair_weight, table],
        [((4, 2, rows, HD), bf16)],
        24,
        8 * 10**9,
    )
    pairs = lax.all_to_all(pairs, "tp", 0, 0, axis_index_groups=same_head)
    queries = [
        kernel(
            query_kernel,
            [gathered, weight, table],
            [((2, heads // 2 * rows, HD), bf16)],
            24,
            4 * rows * width * local,
        )[0]
        for weight in (own_w_query, other_w_query)
    ]
    def partial_output(tick):
        half = block((1, heads // 2 * rows, HD), (tick, 0, 0))
        pair = block((4, 1, rows, HD), (0, tick, 0, 0))
        cache = block(cache_own.shape)
        return kernel(
            attend_kernel,
            [prefix_len, info, *queries, pairs, *caches, own_w_out, other_w_out],
            [((chips, tokens, width), bf16)],
            24,
            2 * rows * heads * HD * (width + 2 * PREFIX),
            [smem] * 2 + [half] * 2 + [pair] + [cache] * 4 + [hbm] * 2,
            [pltpu.VMEM((2, *own_w_out.shape), bf16), pltpu.SemaphoreType.DMA((2,))],
        )[0]

    def collected(partial):
        partial = lax.all_to_all(partial, "tp", 0, 0, axis_index_groups=same_core)
        return jnp.sum(partial.astype(f32), axis=0).astype(bf16)

    early_output = to_next_section(collected(partial_output(0)))
    output = collected(partial_output(1))
    final_carried = (earlier[:, :width].astype(f32) + early_output.astype(f32)).astype(bf16)
    return (final_carried[None], output[None])


def solution(mesh):
    in_specs = (
        P("segment", "tp", None),
        P("segment", "tp", None),
        P("segment"),
        P("segment"),
        P("segment", None),
        P("segment", None, "tp"),
        P("segment", None, "tp"),
        P("segment", "tp", None),
        P("segment", "tp", None),
    )
    out_specs = (P("segment", "tp", None), P("segment", "tp", None))
    return jax.shard_map(shards, mesh=mesh, in_specs=in_specs, out_specs=out_specs, check_vma=False)
```

time: 280 us -> 89.6 us (0.32)
  the two profiles are of different devices: /device:TPU:24 before, /device:TPU:34 now
where the time goes in v2:
time: 89.6 us; the launch traced here: 88.5 us
  starting transfers between devices  46 us (51%)
  Pallas kernels  18.6 us (21%)
  waiting for transfers between devices  15.9 us (18%)
  local copies, waits for them, and re-layouts  3.28 us (4%)
  other arithmetic  2.54 us (3%)
  between operations  2.19 us (2%)
    pallas_call x8, Pallas kernels, kernel(): pl.pallas_call(body, grid=(1,), out_shape=[jax.ShapeDtypeStruct(shape, dt...  18.6 us
    ppermute x6, starting transfers between devices, swapped(): lax.ppermute(array, 'tp', [(i, i ^ bit) for i in range(lax.axis_size('tp'...  14.8 us
    all_to_all x2, starting transfers between devices, collected(): partial = lax.all_to_all(partial, 'tp', 0, 0, axis_index_groups=same_core)  11.6 us
    ppermute x2, starting transfers between devices, to_next_section(): lax.ppermute(array, 'segment', [(i, i + 1) for i in range(sections - 1)])  10.4 us
    ppermute x2, waiting for transfers between devices, to_next_section(): lax.ppermute(array, 'segment', [(i, i + 1) for i in range(sections - 1)])  7.54 us
    all_to_all x2, waiting for transfers between devices, collected(): partial = lax.all_to_all(partial, 'tp', 0, 0, axis_index_groups=same_core)  7 us
    all_to_all x1, starting transfers between devices, shards(): gathered = lax.all_to_all(normed, 'tp', 0, 0, axis_index_groups=same_core)  5.78 us
    all_to_all x1, starting transfers between devices, shards(): pairs = lax.all_to_all(pairs, 'tp', 0, 0, axis_index_groups=same_head)  3.32 us
  transfers between devices with their start and end apart: 12, of which 5 were waited for; matrix products, arithmetic and copies ran while one was open for 2% of the time, Pallas kernels for 14%

profile of v2, /device:TPU:34, one launch (start us, length us, event | category | flops | bytes accessed | tf_op | source)
XLA Modules:
  0.0 88.5 jit_solution(7992819022012325325)
XLA Ops:
  1.3 1.5 %shard_map.140 = bf16[8,4224]{1,0:T(8,128)(2,1)} custom-call(s32[1]{0:T(128)S(6)} %copy.15.span_ref, bf16[8,4096]{1,0:T(8,128)(2,1)} %bitcast.25, bf16[8,4096]{1,0:T(8,128)(2,1)} %bitcast.24), custom_call_target="tpu_custom_call" | custom-call | flops 1048576 | bytes 16384 | tf_op jit(solution)/shard_map/pallas_call | solution.py:200
  2.8 6.1 %collective-permute-start = (bf16[8,4224]{1,0:T(8,128)(2,1)}, bf16[8,4224]{1,0:T(8,128)(2,1)S(1)}, u32[]{:S(2)}, u32[]{:S(2)}) collective-permute-start(bf16[8,4224]{1,0:T(8,128)(2,1)} %shard_map.140), channel_id=1, source_target_pairs={{0,16},{16,32},{32,48},{48,64},{64,80},{80,96},{96,112},{112,128},... | collective-permute-start | bytes 202760 | tf_op jit(solution)/shard_map/ppermute | solution.py:169
  8.9 4.3 %collective-permute-start.1 = (bf16[384,256]{1,0:T(8,128)(2,1)}, bf16[384,256]{1,0:T(8,128)(2,1)}, u32[]{:S(2)}, u32[]{:S(2)}) collective-permute-start(bf16[384,256]{1,0:T(8,128)(2,1)} %bitcast.4.own), channel_id=1, source_target_pairs={{0,2},{1,3},{2,0},{3,1},{4,6},{5,7},{6,4},{7,5},{8,10},{9,11},{10,... | collective-permute-start | bytes 589832 | tf_op jit(solution)/shard_map/ppermute | solution.py:164
  13.2 4.2 %collective-permute-done.earlier_ref = bf16[8,4224]{1,0:T(8,128)(2,1)S(1)} collective-permute-done((bf16[8,4224]{1,0:T(8,128)(2,1)}, bf16[8,4224]{1,0:T(8,128)(2,1)S(1)}, u32[]{:S(2)}, u32[]{:S(2)}) %collective-permute-start) | collective-permute-done | bytes 67616 | tf_op jit(solution)/shard_map/ppermute | solution.py:169
  18.0 2.1 %shard_map.141 = bf16[8,16,4096]{2,1,0:T(8,128)(2,1)} custom-call(bf16[8,4096]{1,0:T(8,128)(2,1)} %bitcast.26, bf16[8,4224]{1,0:T(8,128)(2,1)} %copy-done.2, bf16[1,4096]{1,0:T(2,128)(2,1)} %gain_ref.1), custom_call_target="tpu_custom_call" | custom-call | flops 10000000000 | bytes 156250000 | tf_op jit(solution)/shard_map/pallas_call | solution.py:200
  20.1 5.8 %all-to-all-start = ((bf16[8,16,4096]{2,1,0:T(8,128)(2,1)}), bf16[8,16,4096]{2,1,0:T(8,128)(2,1)S(1)}, u32[]{:S(2)}, u32[]{:S(2)}) async-start(bf16[8,16,4096]{2,1,0:T(8,128)(2,1)} %shard_map.141), calls=%async_computation | async-start | bytes 2097152 | tf_op jit(solution)/shard_map/all_to_all | solution.py:224
  25.9 1.9 %collective-permute-start.2 = (bf16[4096,256]{1,0:T(8,128)(2,1)}, bf16[4096,256]{1,0:T(8,128)(2,1)}, u32[]{:S(2)}, u32[]{:S(2)}) collective-permute-start(bf16[4096,256]{1,0:T(8,128)(2,1)} %bitcast.20), channel_id=1, source_target_pairs={{0,1},{1,0},{2,3},{3,2},{4,5},{5,4},{6,7},{7,6},{8,9},{9,8},{10,11... | collective-permute-start | bytes 6291464 | tf_op jit(solution)/shard_map/ppermute | solution.py:164
  27.8 2.4 %collective-permute-start.6 = (bf16[256,4096]{1,0:T(8,128)(2,1)S(1)}, bf16[256,4096]{1,0:T(8,128)(2,1)}, u32[]{:S(2)}, u32[]{:S(2)}) collective-permute-start(bf16[256,4096]{1,0:T(8,128)(2,1)S(1)} %bitcast.17), channel_id=1, source_target_pairs={{0,1},{1,0},{2,3},{3,2},{4,5},{5,4},{6,7},{7,6},{8,9},{9,8},{10,11... | collective-permute-start | bytes 6291464 | tf_op jit(solution)/shard_map/ppermute | solution.py:164
  30.2 1.9 %collective-permute-start.3 = (bf16[64,4096]{1,0:T(8,128)(2,1)}, bf16[64,4096]{1,0:T(8,128)(2,1)}, u32[]{:S(2)}, u32[]{:S(2)}) collective-permute-start(bf16[64,4096]{1,0:T(8,128)(2,1)} %bitcast.22), channel_id=1, source_target_pairs={{0,1},{1,0},{2,3},{3,2},{4,5},{5,4},{6,7},{7,6},{8,9},{9,8},{10,11... | collective-permute-start | bytes 1572872 | tf_op jit(solution)/shard_map/ppermute | solution.py:164
  32.3 2.4 %collective-permute-start.4 = (bf16[384,256]{1,0:T(8,128)(2,1)}, bf16[384,256]{1,0:T(8,128)(2,1)}, u32[]{:S(2)}, u32[]{:S(2)}) collective-permute-start(bf16[384,256]{1,0:T(8,128)(2,1)} %bitcast.4.own), channel_id=1, source_target_pairs={{0,1},{1,0},{2,3},{3,2},{4,5},{5,4},{6,7},{7,6},{8,9},{9,8},{10,11... | collective-permute-start | bytes 589832 | tf_op jit(solution)/shard_map/ppermute | solution.py:164
  34.7 1.9 %collective-permute-start.5 = (bf16[384,256]{1,0:T(8,128)(2,1)}, bf16[384,256]{1,0:T(8,128)(2,1)}, u32[]{:S(2)}, u32[]{:S(2)}) collective-permute-start(bf16[384,256]{1,0:T(8,128)(2,1)} %collective-permute-done.1.from_z), channel_id=1, source_target_pairs={{0,1},{1,0},{2,3},{3,2},{4,5},{5,4},{6,7},{7,6},{8,9},{9,8},{10,11... | collective-permute-start | bytes 589832 | tf_op jit(solution)/shard_map/ppermute | solution.py:164
  37.3 1.3 %all-to-all-done = bf16[8,16,4096]{2,1,0:T(8,128)(2,1)S(1)} async-done(((bf16[8,16,4096]{2,1,0:T(8,128)(2,1)}), bf16[8,16,4096]{2,1,0:T(8,128)(2,1)S(1)}, u32[]{:S(2)}, u32[]{:S(2)}) %all-to-all-start) | async-done | bytes 1048608 | tf_op jit(solution)/shard_map/all_to_all | solution.py:224
  39.7 2.3 %shard_map.145 = bf16[4,2,64,128]{3,2,1,0:T(8,128)(2,1)} custom-call(s32[2]{0:T(128)S(1)} %pad_add_fusion.info_ref, bf16[128,4096]{1,0:T(8,128)(2,1)S(1)} %bitcast.14, bf16[64,4096]{1,0:T(8,128)(2,1)S(1)} %bitcast.23, bf16[64,4096]{1,0:T(8,128)(2,1)} %collective-permute-done.3.other_ref, f32[2,2,64,128]{3,2,1,0:T(8,128)S(1)} %shard_map.142.table_ref), custom_call_target="tpu_custom_call" | custom-call | flops 8000000000 | bytes 125000000 | tf_op jit(solution)/shard_map/pallas_call | solution.py:200
  41.9 3.3 %all-to-all-start.1 = ((bf16[4,2,64,128]{3,2,1,0:T(8,128)(2,1)}), bf16[4,2,64,128]{3,2,1,0:T(8,128)(2,1)S(1)}, u32[]{:S(2)}, u32[]{:S(2)}) async-start(bf16[4,2,64,128]{3,2,1,0:T(8,128)(2,1)} %shard_map.145), calls=%async_computation.1 | async-start | bytes 262144 | tf_op jit(solution)/shard_map/all_to_all | solution.py:250
  45.9 1.6 %copy-done.1 = bf16[1,4096,256]{2,1,0:T(8,128)(2,1)S(1)} copy-done((bf16[1,4096,256]{2,1,0:T(8,128)(2,1)S(1)}, bf16[1,4096,256]{2,1,0:T(8,128)(2,1)}, u32[]{:S(2)}) %copy-start.1) | copy-done | bytes 2097176
  48.1 2.1 %shard_map.144.q_other = bf16[2,128,128]{2,1,0:T(8,128)(2,1)S(1)} custom-call(bf16[128,4096]{1,0:T(8,128)(2,1)S(1)} %bitcast.16, bf16[4096,256]{1,0:T(8,128)(2,1)} %collective-permute-done.2.weight_ref, f32[2,2,64,128]{3,2,1,0:T(8,128)S(1)} %shard_map.142.table_ref), custom_call_target="tpu_custom_call" | custom-call | flops 268435456 | bytes 4194304 | tf_op jit(solution)/shard_map/pallas_call | solution.py:200
  50.2 4.8 %shard_map.146 = bf16[8,8,4096]{2,1,0:T(8,128)(2,1)} custom-call(s32[1]{0:T(128)S(6)} %copy.16.length_ref, s32[2]{0:T(128)S(1)} %pad_add_fusion.info_ref, bf16[2,128,128]{2,1,0:T(8,128)(2,1)S(1)} %shard_map.143.q_own, bf16[2,128,128]{2,1,0:T(8,128)(2,1)S(1)} %shard_map.144.q_other, bf16[4,2,64,128]{3,2,1,0:T(8,128)(2,1)S(1)} %all-to-all-done.1.kv_ref, ...), custom_call_target="tpu_custom_call" | custom-call | flops 469762048 | bytes 7340032 | tf_op jit(solution)/shard_map/pallas_call | solution.py:200
  55.0 6.1 %all-to-all-start.2 = ((bf16[8,8,4096]{2,1,0:T(8,128)(2,1)}), bf16[8,8,4096]{2,1,0:T(8,128)(2,1)}, u32[]{:S(2)}, u32[]{:S(2)}) async-start(bf16[8,8,4096]{2,1,0:T(8,128)(2,1)} %shard_map.146), calls=%async_computation.2 | async-start | bytes 1048576 | tf_op jit(solution)/shard_map/all_to_all | solution.py:276
  61.1 4.8 %shard_map.147 = bf16[8,8,4096]{2,1,0:T(8,128)(2,1)} custom-call(s32[1]{0:T(128)S(6)} %copy.16.length_ref, s32[2]{0:T(128)S(1)} %pad_add_fusion.info_ref, bf16[2,128,128]{2,1,0:T(8,128)(2,1)S(1)} %shard_map.143.q_own, bf16[2,128,128]{2,1,0:T(8,128)(2,1)S(1)} %shard_map.144.q_other, bf16[4,2,64,128]{3,2,1,0:T(8,128)(2,1)S(1)} %all-to-all-done.1.kv_ref, ...), custom_call_target="tpu_custom_call" | custom-call | flops 469762048 | bytes 7340032 | tf_op jit(solution)/shard_map/pallas_call | solution.py:200
  65.9 4.3 %all-to-all-done.2 = bf16[8,8,4096]{2,1,0:T(8,128)(2,1)} async-done(((bf16[8,8,4096]{2,1,0:T(8,128)(2,1)}), bf16[8,8,4096]{2,1,0:T(8,128)(2,1)}, u32[]{:S(2)}, u32[]{:S(2)}) %all-to-all-start.2) | async-done | bytes 524320 | tf_op jit(solution)/shard_map/all_to_all | solution.py:276
  70.2 5.5 %all-to-all-start.3 = ((bf16[8,8,4096]{2,1,0:T(8,128)(2,1)}), bf16[8,8,4096]{2,1,0:T(8,128)(2,1)S(1)}, u32[]{:S(2)}, u32[]{:S(2)}) async-start(bf16[8,8,4096]{2,1,0:T(8,128)(2,1)} %shard_map.147), calls=%async_computation.3 | async-start | bytes 1048576 | tf_op jit(solution)/shard_map/all_to_all | solution.py:276
  76.8 4.3 %collective-permute-start.7 = (bf16[8,4096]{1,0:T(8,128)(2,1)S(1)}, bf16[8,4096]{1,0:T(8,128)(2,1)S(1)}, u32[]{:S(2)}, u32[]{:S(2)}) collective-permute-start(bf16[8,4096]{1,0:T(8,128)(2,1)S(1)} %reduce_sum.24), channel_id=1, source_target_pairs={{0,16},{16,32},{32,48},{48,64},{64,80},{80,96},{96,112},{112,128},... | collective-permute-start | bytes 196616 | tf_op jit(solution)/shard_map/ppermute | solution.py:169
  81.2 2.7 %all-to-all-done.3 = bf16[8,8,4096]{2,1,0:T(8,128)(2,1)S(1)} async-done(((bf16[8,8,4096]{2,1,0:T(8,128)(2,1)}), bf16[8,8,4096]{2,1,0:T(8,128)(2,1)S(1)}, u32[]{:S(2)}, u32[]{:S(2)}) %all-to-all-start.3) | async-done | bytes 524320 | tf_op jit(solution)/shard_map/all_to_all | solution.py:276
  84.6 3.3 %collective-permute-done.7 = bf16[8,4096]{1,0:T(8,128)(2,1)S(1)} collective-permute-done((bf16[8,4096]{1,0:T(8,128)(2,1)S(1)}, bf16[8,4096]{1,0:T(8,128)(2,1)S(1)}, u32[]{:S(2)}, u32[]{:S(2)}) %collective-permute-start.7) | collective-permute-done | bytes 65568 | tf_op jit(solution)/shard_map/ppermute | solution.py:169
  (32 shorter events, 5.4 us)
Async XLA Ops:
  2.8 14.6 %collective-permute-start = (bf16[8,4224]{1,0:T(8,128)(2,1)}, bf16[8,4224]{1,0:T(8,128)(2,1)S(1)}, u32[]{:S(2)}, u32[]{:S(2)}) collective-permute-start(bf16[8,4224]{1,0:T(8,128)(2,1)} %shard_map.140), channel_id=1, source_target_pairs={{0,16},{16,32},{32,48},{48,64},{64,80},{80,96},{96,112},{112,128},... | collective-permute-start | bytes 202760 | tf_op jit(solution)/shard_map/ppermute | solution.py:169
  8.9 11.3 %collective-permute-start.1 = (bf16[384,256]{1,0:T(8,128)(2,1)}, bf16[384,256]{1,0:T(8,128)(2,1)}, u32[]{:S(2)}, u32[]{:S(2)}) collective-permute-start(bf16[384,256]{1,0:T(8,128)(2,1)} %bitcast.4.own), channel_id=1, source_target_pairs={{0,2},{1,3},{2,0},{3,1},{4,6},{5,7},{6,4},{7,5},{8,10},{9,11},{10,... | collective-permute-start | bytes 589832 | tf_op jit(solution)/shard_map/ppermute | solution.py:164
  17.4 0.6 copy-start.2
  18.0 18.6 %copy-start.5 = (f32[2,64,128]{2,1,0:T(8,128)S(1)}, f32[2,64,128]{2,1,0:T(8,128)}, u32[]{:S(2)}) copy-start(f32[2,64,128]{2,1,0:T(8,128)} %constant.44.clone.cos_tok) | copy-start | bytes 196612
  18.0 18.6 %copy-start.6 = (f32[2,64,128]{2,1,0:T(8,128)S(1)}, f32[2,64,128]{2,1,0:T(8,128)}, u32[]{:S(2)}) copy-start(f32[2,64,128]{2,1,0:T(8,128)} %constant.45.clone.sin_tok) | copy-start | bytes 196612
  18.0 18.6 %copy-start.7 = (f32[64,128]{1,0:T(8,128)S(1)}, f32[64,128]{1,0:T(8,128)}, u32[]{:S(2)}) copy-start(f32[64,128]{1,0:T(8,128)} %constant.46.clone.cos_span) | copy-start | bytes 98308
  18.0 18.6 %copy-start.8 = (f32[64,128]{1,0:T(8,128)S(1)}, f32[64,128]{1,0:T(8,128)}, u32[]{:S(2)}) copy-start(f32[64,128]{1,0:T(8,128)} %constant.47.clone.sin_span) | copy-start | bytes 98308
  20.1 7.7 %copy-start = (bf16[1,256,4096]{2,1,0:T(8,128)(2,1)S(1)}, bf16[1,256,4096]{2,1,0:T(8,128)(2,1)}, u32[]{:S(2)}) copy-start(bf16[1,256,4096]{2,1,0:T(8,128)(2,1)} %param.20) | copy-start | bytes 6291460
  20.1 16.6 %copy-start.3 = (bf16[8,4224]{1,0:T(8,128)(2,1)S(1)}, bf16[8,4224]{1,0:T(8,128)(2,1)}, u32[]{:S(2)}) copy-start(bf16[8,4224]{1,0:T(8,128)(2,1)} %copy-done.2) | copy-start | bytes 202756
  20.1 18.5 %all-to-all-start = ((bf16[8,16,4096]{2,1,0:T(8,128)(2,1)}), bf16[8,16,4096]{2,1,0:T(8,128)(2,1)S(1)}, u32[]{:S(2)}, u32[]{:S(2)}) async-start(bf16[8,16,4096]{2,1,0:T(8,128)(2,1)} %shard_map.141), calls=%async_computation | async-start | bytes 2097152 | tf_op jit(solution)/shard_map/all_to_all | solution.py:224
  25.9 22.1 %collective-permute-start.2 = (bf16[4096,256]{1,0:T(8,128)(2,1)}, bf16[4096,256]{1,0:T(8,128)(2,1)}, u32[]{:S(2)}, u32[]{:S(2)}) collective-permute-start(bf16[4096,256]{1,0:T(8,128)(2,1)} %bitcast.20), channel_id=1, source_target_pairs={{0,1},{1,0},{2,3},{3,2},{4,5},{5,4},{6,7},{7,6},{8,9},{9,8},{10,11... | collective-permute-start | bytes 6291464 | tf_op jit(solution)/shard_map/ppermute | solution.py:164
  27.8 22.4 %collective-permute-start.6 = (bf16[256,4096]{1,0:T(8,128)(2,1)S(1)}, bf16[256,4096]{1,0:T(8,128)(2,1)}, u32[]{:S(2)}, u32[]{:S(2)}) collective-permute-start(bf16[256,4096]{1,0:T(8,128)(2,1)S(1)} %bitcast.17), channel_id=1, source_target_pairs={{0,1},{1,0},{2,3},{3,2},{4,5},{5,4},{6,7},{7,6},{8,9},{9,8},{10,11... | collective-permute-start | bytes 6291464 | tf_op jit(solution)/shard_map/ppermute | solution.py:164
  30.2 7.0 %collective-permute-start.3 = (bf16[64,4096]{1,0:T(8,128)(2,1)}, bf16[64,4096]{1,0:T(8,128)(2,1)}, u32[]{:S(2)}, u32[]{:S(2)}) collective-permute-start(bf16[64,4096]{1,0:T(8,128)(2,1)} %bitcast.22), channel_id=1, source_target_pairs={{0,1},{1,0},{2,3},{3,2},{4,5},{5,4},{6,7},{7,6},{8,9},{9,8},{10,11... | collective-permute-start | bytes 1572872 | tf_op jit(solution)/shard_map/ppermute | solution.py:164
  32.3 17.9 %collective-permute-start.4 = (bf16[384,256]{1,0:T(8,128)(2,1)}, bf16[384,256]{1,0:T(8,128)(2,1)}, u32[]{:S(2)}, u32[]{:S(2)}) collective-permute-start(bf16[384,256]{1,0:T(8,128)(2,1)} %bitcast.4.own), channel_id=1, source_target_pairs={{0,1},{1,0},{2,3},{3,2},{4,5},{5,4},{6,7},{7,6},{8,9},{9,8},{10,11... | collective-permute-start | bytes 589832 | tf_op jit(solution)/shard_map/ppermute | solution.py:164
  34.7 15.5 %collective-permute-start.5 = (bf16[384,256]{1,0:T(8,128)(2,1)}, bf16[384,256]{1,0:T(8,128)(2,1)}, u32[]{:S(2)}, u32[]{:S(2)}) collective-permute-start(bf16[384,256]{1,0:T(8,128)(2,1)} %collective-permute-done.1.from_z), channel_id=1, source_target_pairs={{0,1},{1,0},{2,3},{3,2},{4,5},{5,4},{6,7},{7,6},{8,9},{9,8},{10,11... | collective-permute-start | bytes 589832 | tf_op jit(solution)/shard_map/ppermute | solution.py:164
  38.6 1.0 %copy-start.9 = (bf16[1,4096,64]{1,2,0:T(8,128)(2,1)S(1)}, bf16[1,4096,64]{1,2,0:T(8,128)(2,1)}, u32[]{:S(2)}) copy-start(bf16[1,4096,64]{1,2,0:T(8,128)(2,1)} %param.19) | copy-start | bytes 1572868
  41.9 8.2 %all-to-all-start.1 = ((bf16[4,2,64,128]{3,2,1,0:T(8,128)(2,1)}), bf16[4,2,64,128]{3,2,1,0:T(8,128)(2,1)S(1)}, u32[]{:S(2)}, u32[]{:S(2)}) async-start(bf16[4,2,64,128]{3,2,1,0:T(8,128)(2,1)} %shard_map.145), calls=%async_computation.1 | async-start | bytes 262144 | tf_op jit(solution)/shard_map/all_to_all | solution.py:250
  45.9 1.6 %copy-start.1 = (bf16[1,4096,256]{2,1,0:T(8,128)(2,1)S(1)}, bf16[1,4096,256]{2,1,0:T(8,128)(2,1)}, u32[]{:S(2)}) copy-start(bf16[1,4096,256]{2,1,0:T(8,128)(2,1)} %param.18) | copy-start | bytes 6291460
  55.0 15.2 %all-to-all-start.2 = ((bf16[8,8,4096]{2,1,0:T(8,128)(2,1)}), bf16[8,8,4096]{2,1,0:T(8,128)(2,1)}, u32[]{:S(2)}, u32[]{:S(2)}) async-start(bf16[8,8,4096]{2,1,0:T(8,128)(2,1)} %shard_map.146), calls=%async_computation.2 | async-start | bytes 1048576 | tf_op jit(solution)/shard_map/all_to_all | solution.py:276
  65.9 22.0 %copy-start.4 = (bf16[8,4224]{1,0:T(8,128)(2,1)S(1)}, bf16[8,4224]{1,0:T(8,128)(2,1)}, u32[]{:S(2)}) copy-start(bf16[8,4224]{1,0:T(8,128)(2,1)} %copy-done.2) | copy-start | bytes 202756
  70.2 13.7 %all-to-all-start.3 = ((bf16[8,8,4096]{2,1,0:T(8,128)(2,1)}), bf16[8,8,4096]{2,1,0:T(8,128)(2,1)S(1)}, u32[]{:S(2)}, u32[]{:S(2)}) async-start(bf16[8,8,4096]{2,1,0:T(8,128)(2,1)} %shard_map.147), calls=%async_computation.3 | async-start | bytes 1048576 | tf_op jit(solution)/shard_map/all_to_all | solution.py:276
  76.8 11.1 %collective-permute-start.7 = (bf16[8,4096]{1,0:T(8,128)(2,1)S(1)}, bf16[8,4096]{1,0:T(8,128)(2,1)S(1)}, u32[]{:S(2)}, u32[]{:S(2)}) collective-permute-start(bf16[8,4096]{1,0:T(8,128)(2,1)S(1)} %reduce_sum.24), channel_id=1, source_target_pairs={{0,16},{16,32},{32,48},{48,64},{64,80},{80,96},{96,112},{112,128},... | collective-permute-start | bytes 196616 | tf_op jit(solution)/shard_map/ppermute | solution.py:169

commit v3 on v2

--- a/solution.py
+++ b/solution.py
@@ -37,8 +37,8 @@
     tokens, width = residual_ref.shape
     carried = residual_ref[...].astype(jnp.float32) + pending_ref[...].astype(jnp.float32)
     out_ref[:, :width] = carried.astype(jnp.bfloat16)
-    index = jnp.full((tokens, out_ref.shape[1] - width), span_ref[0], jnp.int32)
-    out_ref[:, width:] = index.astype(jnp.float32).astype(jnp.bfloat16)
+    index = span_ref[...].astype(jnp.float32).astype(jnp.bfloat16)
+    out_ref[:, width:] = jnp.broadcast_to(index, (tokens, out_ref.shape[1] - width))
 
 
 def normalised(rows_ref, gain_ref):
@@ -54,13 +54,13 @@
         out_ref[copy] = normed
 
 
-def table_kernel(span_ref, info_ref, earlier_ref, cos_tok, sin_tok, cos_span, sin_span, out_ref):
+def table_kernel(info_ref, span_ref, earlier_ref, cos_tok, sin_tok, cos_span, sin_span, out_ref):
     core = info_ref[0]
     late = earlier_ref[:, -HD:].astype(jnp.float32)[:1].astype(jnp.int32)
     spans = lax.broadcasted_iota(jnp.int32, cos_span.shape, 0)
     low = lax.broadcasted_iota(jnp.int32, out_ref.shape[2:], 1) < HD // 2
     cos_b, sin_b = cos_tok[core], sin_tok[core]
-    for tick, index in enumerate((span_ref[0], late)):
+    for tick, index in enumerate((span_ref[...], late)):
         cos_a, sin_a = [
             jnp.sum(jnp.where(spans == index, table[...], 0.0), axis=0, keepdims=True)
             for table in (cos_span, sin_span)
@@ -80,13 +80,27 @@
     return (values * table_ref[0, tick] + turned).astype(jnp.bfloat16)
 
 
-def query_kernel(rows_ref, weight_ref, table_ref, q_ref):
-    queries = jnp.dot(rows_ref[...], weight_ref[...], preferred_element_type=jnp.float32)
+def query_kernel(rows_ref, own_hbm, other_hbm, table_ref, q_ref, weight_ref, sems):
+    slices = []
+    for side, weight_hbm in enumerate((own_hbm, other_hbm)):
+        for head in range(weight_hbm.shape[1] // HD):
+            columns = pl.ds(head * HD, HD)
+            at = len(slices)
+            slices.append(
+                pltpu.make_async_copy(
+                    weight_hbm.at[:, columns], weight_ref.at[side, :, columns], sems.at[at]
+                )
+            )
+            slices[at].start()
     rows = rows_ref.shape[0] // 2
-    for tick in range(2):
-        for head in range(queries.shape[1] // HD):
-            values = of_tick(queries[:, head * HD : (head + 1) * HD], tick)
-            q_ref[tick, pl.ds(head * rows, rows), :] = rotated(values, table_ref, tick)
+    heads = len(slices) // 2
+    for at in range(len(slices)):
+        slices[at].wait()
+        weight = weight_ref[at // heads, :, at % heads * HD : (at % heads + 1) * HD]
+        queries = jnp.dot(rows_ref[...], weight, preferred_element_type=jnp.float32)
+        for tick in range(2):
+            values = of_tick(queries, tick)
+            q_ref[tick, pl.ds(at * rows, rows), :] = rotated(values, table_ref, tick)
 
 
 def pair_kernel(info_ref, rows_ref, own_ref, other_ref, table_ref, kv_ref):
@@ -104,19 +118,21 @@
 
 
 def attend_kernel(
-    length_ref, info_ref, q_own, q_other, kv_ref, own, from_z, from_core, from_both,
-    wout_own_any, wout_other_any, out_ref, wout_ref, sems,
+    info_ref, length_ref, kv_ref, wout_own, q_hbm, own, from_z, from_core, from_both, wout_hbm,
+    out_ref, q_ref, cache_ref, wout_other, sems, *, tick,
 ):
-    weight_copies = [
-        pltpu.make_async_copy(source, wout_ref.at[side], sems.at[side])
-        for side, source in enumerate((wout_own_any, wout_other_any))
-    ]
-    for copy in weight_copies:
+    copies = [pltpu.make_async_copy(q_hbm.at[tick], q_ref, sems.at[0])]
+    for at, cache in enumerate((own, from_z, from_core, from_both)):
+        copies.append(pltpu.make_async_copy(cache, cache_ref.at[at], sems.at[1 + at]))
+    copies.append(pltpu.make_async_copy(wout_hbm, wout_other, sems.at[5]))
+    for copy in copies:
         copy.start()
+    for copy in copies[:5]:
+        copy.wait()
     core, z_place = info_ref[0], info_ref[1]
     chips, tokens, width = out_ref.shape
     rows = chips * tokens
-    queries = jnp.concatenate([q_own[0], q_other[0]], axis=0)
+    queries = q_ref[...]
 
     def token(index, side):
         return ((index % rows // tokens) * 2 + side) * tokens + index % tokens
@@ -126,13 +142,13 @@
     allowed = [token(key, key // rows) <= row_token]
     keys = [jnp.concatenate([kv_ref[0, 0], kv_ref[1, 0]], axis=0)]
     values = [jnp.concatenate([kv_ref[2, 0], kv_ref[3, 0]], axis=0)]
-    block = own.shape[0]
+    block = cache_ref.shape[1]
     slot = lax.broadcasted_iota(jnp.int32, (1, block), 1)
     places = [(z, c) for c in (core, 1 - core) for z in (z_place, 1 - z_place)]
-    for cache_ref, (z, c) in zip((own, from_z, from_core, from_both), places):
-        keys.append(cache_ref[:, :HD])
-        values.append(cache_ref[:, HD:])
-        allowed.append((z * 2 + c) * block + slot < length_ref[0])
+    for at, (z, c) in enumerate(places):
+        keys.append(cache_ref[at, :, :HD])
+        values.append(cache_ref[at, :, HD:])
+        allowed.append((z * 2 + c) * block + slot < length_ref[...])
 
     scores = []
     for key, seen in zip(keys, allowed):
@@ -148,14 +164,13 @@
     heads = [result[at : at + rows] for at in range(0, queries.shape[0], rows)]
     half = len(heads) // 2
     sides = [jnp.concatenate(heads[:half], axis=1), jnp.concatenate(heads[half:], axis=1)]
-    for copy in weight_copies:
-        copy.wait()
+    copies[5].wait()
     step = 1024
     for left in range(0, width, step):
         columns = pl.ds(left, step)
         part = sum(
-            jnp.dot(sides[side], wout_ref[side, :, columns], preferred_element_type=jnp.float32)
-            for side in range(2)
+            jnp.dot(side, wout_ref[:, columns], preferred_element_type=jnp.float32)
+            for side, wout_ref in zip(sides, (wout_own, wout_other))
         )
         out_ref[:, :, columns] = part.reshape(chips, tokens, step).astype(jnp.bfloat16)
 
@@ -187,7 +202,6 @@
     same_core = [list(range(c, tp_size, 2)) for c in range(2)]
     same_head = [list(range(i, i + 4)) for i in range(0, tp_size, 4)]
     smem = pl.BlockSpec(memory_space=pltpu.SMEM)
-    hbm = pl.BlockSpec(memory_space=pl.ANY)
     bf16, f32 = jnp.bfloat16, jnp.float32
     cos_tok, sin_tok, cos_span, sin_span = [jnp.asarray(t) for t in rope_tables()]
 
@@ -200,25 +214,36 @@
         return pl.pallas_call(
             body,
             grid=(1,),
-            out_shape=[jax.ShapeDtypeStruct(shape, dtype) for shape, dtype in outs],
+            out_shape=outs,
             in_specs=specs,
-            out_specs=[block(shape) for shape, _ in outs],
+            out_specs=[block(out.shape) for out in outs],
             scratch_shapes=scratch,
             compiler_params=pltpu.CompilerParams(vmem_limit_bytes=limit * MIB),
-            cost_estimate=pl.CostEstimate(flops=flops, bytes_accessed=flops // 64, transcendentals=0),
+            cost_estimate=pl.CostEstimate(
+                flops=flops, bytes_accessed=flops // 64, transcendentals=0
+            ),
         )(*inputs)
 
+    def in_vmem(array):
+        return pltpu.with_memory_space_constraint(array, pltpu.VMEM)
+
+    def in_hbm(array):
+        return pltpu.with_memory_space_constraint(array, pltpu.HBM)
+
+    span, length = span_index[:, None], prefix_len[:, None]
     (carried,) = kernel(
-        carry_kernel, [span_index, residual[0], pending[0]], [((tokens, width + HD), bf16)], 60
+        carry_kernel,
+        [span, in_hbm(residual[0]), in_hbm(pending[0])],
+        [pltpu.VMEM((tokens, width + HD), bf16)],
+        16,
     )
     earlier = to_next_section(carried)
     cache_z = swapped(prefix_cache[0], 2)
     (normed,) = kernel(
         norm_kernel,
-        [residual[0], earlier, norm_gain],
-        [((chips, 2 * tokens, width), bf16)],
-        60,
-        10 * 10**9,
+        [in_hbm(residual[0]), in_vmem(earlier), in_hbm(norm_gain)],
+        [pltpu.HBM((chips, 2 * tokens, width), bf16)],
+        16,
     )
     normed, cache_z = after(normed, cache_z)
     gathered = lax.all_to_all(normed, "tp", 0, 0, axis_index_groups=same_core)
@@ -227,8 +252,8 @@
     _, late_earlier = after(normed, earlier)
     (table,) = kernel(
         table_kernel,
-        [span_index, info, late_earlier, cos_tok, sin_tok, cos_span, sin_span],
-        [((2, 2, rows, HD), f32)],
+        [info, span, late_earlier, cos_tok, sin_tok, cos_span, sin_span],
+        [jax.ShapeDtypeStruct((2, 2, rows, HD), f32)],
         16,
         flops=0,
     )
@@ -242,34 +267,39 @@
 
     (pairs,) = kernel(
         pair_kernel,
-        [info, gathered, pair_weight, other_pair_weight, table],
-        [((4, 2, rows, HD), bf16)],
+        [info, gathered, in_hbm(pair_weight), in_hbm(other_pair_weight), table],
+        [pltpu.HBM((4, 2, rows, HD), bf16)],
         24,
-        8 * 10**9,
+        2 * 10**9,
     )
     pairs = lax.all_to_all(pairs, "tp", 0, 0, axis_index_groups=same_head)
-    queries = [
-        kernel(
-            query_kernel,
-            [gathered, weight, table],
-            [((2, heads // 2 * rows, HD), bf16)],
-            24,
-            4 * rows * width * local,
-        )[0]
-        for weight in (own_w_query, other_w_query)
-    ]
+    anywhere = pl.BlockSpec(memory_space=pl.ANY)
+    (queries,) = kernel(
+        query_kernel,
+        [gathered, in_hbm(own_w_query), in_hbm(other_w_query), table],
+        [pltpu.HBM((2, heads * rows, HD), bf16)],
+        24,
+        4 * rows * heads * HD * width,
+        [block(gathered.shape), anywhere, anywhere, block(table.shape)],
+        [pltpu.VMEM((2, *own_w_query.shape), bf16), pltpu.SemaphoreType.DMA((heads,))],
+    )
+
     def partial_output(tick):
-        half = block((1, heads // 2 * rows, HD), (tick, 0, 0))
         pair = block((4, 1, rows, HD), (0, tick, 0, 0))
-        cache = block(cache_own.shape)
+        far = [in_hbm(array) for array in (queries, *caches, other_w_out)]
         return kernel(
-            attend_kernel,
-            [prefix_len, info, *queries, pairs, *caches, own_w_out, other_w_out],
-            [((chips, tokens, width), bf16)],
+            functools.partial(attend_kernel, tick=tick),
+            [info, length, pairs, own_w_out, *far],
+            [pltpu.HBM((chips, tokens, width), bf16)],
             24,
             2 * rows * heads * HD * (width + 2 * PREFIX),
-            [smem] * 2 + [half] * 2 + [pair] + [cache] * 4 + [hbm] * 2,
-            [pltpu.VMEM((2, *own_w_out.shape), bf16), pltpu.SemaphoreType.DMA((2,))],
+            [smem, block(length.shape), pair, block(own_w_out.shape)] + [anywhere] * 6,
+            [
+                pltpu.VMEM((heads * rows, HD), bf16),
+                pltpu.VMEM((4, *cache_own.shape), bf16),
+                pltpu.VMEM(own_w_out.shape, bf16),
+                pltpu.SemaphoreType.DMA((6,)),
+            ],
         )[0]
 
     def collected(partial):

time: 89.6 us -> 87 us (0.971)
  waiting for transfers between devices: 15.9 us -> 20.3 us
  starting transfers between devices: 46 us -> 42.6 us
  local copies, waits for them, and re-layouts: 3.28 us -> 0.72 us
  other arithmetic: 2.54 us -> 1.5 us
    unnamed x20 -> x12, local copies, waits for them, and re-layouts: 3.28 us -> 0.72 us
    all_to_all x2, waiting for transfers between devices: 7 us -> 9.54 us  [collected(): partial = lax.all_to_all(partial, 'tp', 0, 0, axis_index_groups=same_core)]
    ppermute x2, starting transfers between devices: 10.4 us -> 8.01 us  [to_next_section(): lax.ppermute(array, 'segment', [(i, i + 1) for i in range(sections - 1)])]
    ppermute x2, waiting for transfers between devices: 7.54 us -> 9.61 us  [to_next_section(): lax.ppermute(array, 'segment', [(i, i + 1) for i in range(sections - 1)])]
    reduce_sum x2, other arithmetic: 1.82 us -> 0.78 us  [collected(): return jnp.sum(partial.astype(f32), axis=0).astype(bf16)]
    all_to_all x1, starting transfers between devices: 5.78 us -> 4.83 us  [shards(): gathered = lax.all_to_all(normed, 'tp', 0, 0, axis_index_groups=same_core)]
    pallas_call x8 -> x7, Pallas kernels: 18.6 us -> 18.8 us  [kernel(): pl.pallas_call(body, grid=(1,), out_shape=outs, in_specs=specs, out_specs...]
  transfers between devices with their start and end apart: 12 -> 12, of which waited for: 5 -> 5; matrix products, arithmetic and copies ran while one was open for 2% -> 1% of each run, Pallas kernels for 14% -> 17%
where the time goes in v3:
time: 87 us; the launch traced here: 86.2 us
  starting transfers between devices  42.6 us (49%)
  waiting for transfers between devices  20.3 us (23%)
  Pallas kernels  18.8 us (22%)
  between operations  2.2 us (3%)
  other arithmetic  1.5 us (2%)
    pallas_call x7, Pallas kernels, kernel(): pl.pallas_call(body, grid=(1,), out_shape=outs, in_specs=specs, out_specs...  18.8 us
    ppermute x6, starting transfers between devices, swapped(): lax.ppermute(array, 'tp', [(i, i ^ bit) for i in range(lax.axis_size('tp'...  15 us
    all_to_all x2, starting transfers between devices, collected(): partial = lax.all_to_all(partial, 'tp', 0, 0, axis_index_groups=same_core)  11.5 us
    ppermute x2, waiting for transfers between devices, to_next_section(): lax.ppermute(array, 'segment', [(i, i + 1) for i in range(sections - 1)])  9.61 us
    all_to_all x2, waiting for transfers between devices, collected(): partial = lax.all_to_all(partial, 'tp', 0, 0, axis_index_groups=same_core)  9.54 us
    ppermute x2, starting transfers between devices, to_next_section(): lax.ppermute(array, 'segment', [(i, i + 1) for i in range(sections - 1)])  8.01 us
    all_to_all x1, starting transfers between devices, shards(): gathered = lax.all_to_all(normed, 'tp', 0, 0, axis_index_groups=same_core)  4.83 us
    all_to_all x1, starting transfers between devices, shards(): pairs = lax.all_to_all(pairs, 'tp', 0, 0, axis_index_groups=same_head)  3.32 us
  transfers between devices with their start and end apart: 12, of which 5 were waited for; matrix products, arithmetic and copies ran while one was open for 1% of the time, Pallas kernels for 17%

profile of v3, /device:TPU:34, one launch (start us, length us, event | category | flops | bytes accessed | tf_op | source)
XLA Modules:
  0.0 86.2 jit_solution(13681767864815661283)
XLA Ops:
  0.7 4.4 %collective-permute-start.1 = (bf16[384,256]{1,0:T(8,128)(2,1)}, bf16[384,256]{1,0:T(8,128)(2,1)S(1)}, u32[]{:S(2)}, u32[]{:S(2)}) collective-permute-start(bf16[384,256]{1,0:T(8,128)(2,1)} %bitcast.27), channel_id=1, source_target_pairs={{0,2},{1,3},{2,0},{3,1},{4,6},{5,7},{6,4},{7,5},{8,10},{9,11},{10,... | collective-permute-start | bytes 589832 | tf_op jit(solution)/shard_map/ppermute | solution.py:179
  5.8 0.9 %shard_map.140 = bf16[8,4224]{1,0:T(8,128)(2,1)S(1)} custom-call(s32[1,1]{1,0:T(1,128)} %bitcast.16.span_ref, bf16[8,4096]{1,0:T(8,128)(2,1)} %bitcast.31, bf16[8,4096]{1,0:T(8,128)(2,1)} %bitcast.33), custom_call_target="tpu_custom_call" | custom-call | flops 1048576 | bytes 16384 | tf_op jit(solution)/shard_map/pallas_call | solution.py:214
  6.7 6.1 %collective-permute-start = (bf16[8,4224]{1,0:T(8,128)(2,1)S(1)}, bf16[8,4224]{1,0:T(8,128)(2,1)S(1)}, u32[]{:S(2)}, u32[]{:S(2)}) collective-permute-start(bf16[8,4224]{1,0:T(8,128)(2,1)S(1)} %shard_map.140), channel_id=1, source_target_pairs={{0,16},{16,32},{32,48},{48,64},{64,80},{80,96},{96,112},{112,128},... | collective-permute-start | bytes 202760 | tf_op jit(solution)/shard_map/ppermute | solution.py:184
  12.8 6.7 %collective-permute-done.earlier_ref = bf16[8,4224]{1,0:T(8,128)(2,1)S(1)} collective-permute-done((bf16[8,4224]{1,0:T(8,128)(2,1)S(1)}, bf16[8,4224]{1,0:T(8,128)(2,1)S(1)}, u32[]{:S(2)}, u32[]{:S(2)}) %collective-permute-start) | collective-permute-done | bytes 67616 | tf_op jit(solution)/shard_map/ppermute | solution.py:184
  19.5 2.0 %shard_map.141 = bf16[8,16,4096]{2,1,0:T(8,128)(2,1)} custom-call(bf16[8,4096]{1,0:T(8,128)(2,1)} %bitcast.32, bf16[8,4224]{1,0:T(8,128)(2,1)S(1)} %collective-permute-done.earlier_ref, bf16[1,4096]{1,0:T(2,128)(2,1)} %gain_ref.1), custom_call_target="tpu_custom_call" | custom-call | flops 1048576 | bytes 16384 | tf_op jit(solution)/shard_map/pallas_call | solution.py:214
  22.2 4.8 %all-to-all-start = ((bf16[8,16,4096]{2,1,0:T(8,128)(2,1)}), bf16[8,16,4096]{2,1,0:T(8,128)(2,1)S(1)}, u32[]{:S(2)}, u32[]{:S(2)}) async-start(bf16[8,16,4096]{2,1,0:T(8,128)(2,1)} %shard_map.141), calls=%async_computation | async-start | bytes 2097152 | tf_op jit(solution)/shard_map/all_to_all | solution.py:249
  27.0 1.9 %collective-permute-start.3 = (bf16[4096,256]{1,0:T(8,128)(2,1)}, bf16[4096,256]{1,0:T(8,128)(2,1)}, u32[]{:S(2)}, u32[]{:S(2)}) collective-permute-start(bf16[4096,256]{1,0:T(8,128)(2,1)} %bitcast.25), channel_id=1, source_target_pairs={{0,1},{1,0},{2,3},{3,2},{4,5},{5,4},{6,7},{7,6},{8,9},{9,8},{10,11... | collective-permute-start | bytes 6291464 | tf_op jit(solution)/shard_map/ppermute | solution.py:179
  29.0 2.4 %collective-permute-start.6 = (bf16[256,4096]{1,0:T(8,128)(2,1)S(1)}, bf16[256,4096]{1,0:T(8,128)(2,1)}, u32[]{:S(2)}, u32[]{:S(2)}) collective-permute-start(bf16[256,4096]{1,0:T(8,128)(2,1)S(1)} %bitcast.20), channel_id=1, source_target_pairs={{0,1},{1,0},{2,3},{3,2},{4,5},{5,4},{6,7},{7,6},{8,9},{9,8},{10,11... | collective-permute-start | bytes 6291464 | tf_op jit(solution)/shard_map/ppermute | solution.py:179
  31.4 1.9 %collective-permute-start.2 = (bf16[64,4096]{1,0:T(8,128)(2,1)}, bf16[64,4096]{1,0:T(8,128)(2,1)}, u32[]{:S(2)}, u32[]{:S(2)}) collective-permute-start(bf16[64,4096]{1,0:T(8,128)(2,1)} %bitcast.35), channel_id=1, source_target_pairs={{0,1},{1,0},{2,3},{3,2},{4,5},{5,4},{6,7},{7,6},{8,9},{9,8},{10,11... | collective-permute-start | bytes 1572872 | tf_op jit(solution)/shard_map/ppermute | solution.py:179
  33.4 2.4 %collective-permute-start.4 = (bf16[384,256]{1,0:T(8,128)(2,1)}, bf16[384,256]{1,0:T(8,128)(2,1)}, u32[]{:S(2)}, u32[]{:S(2)}) collective-permute-start(bf16[384,256]{1,0:T(8,128)(2,1)} %bitcast.28), channel_id=1, source_target_pairs={{0,1},{1,0},{2,3},{3,2},{4,5},{5,4},{6,7},{7,6},{8,9},{9,8},{10,11... | collective-permute-start | bytes 589832 | tf_op jit(solution)/shard_map/ppermute | solution.py:179
  35.8 1.9 %collective-permute-start.5 = (bf16[384,256]{1,0:T(8,128)(2,1)}, bf16[384,256]{1,0:T(8,128)(2,1)}, u32[]{:S(2)}, u32[]{:S(2)}) collective-permute-start(bf16[384,256]{1,0:T(8,128)(2,1)} %copy-done.5), channel_id=1, source_target_pairs={{0,1},{1,0},{2,3},{3,2},{4,5},{5,4},{6,7},{7,6},{8,9},{9,8},{10,11... | collective-permute-start | bytes 589832 | tf_op jit(solution)/shard_map/ppermute | solution.py:179
  38.4 1.2 %all-to-all-done = bf16[8,16,4096]{2,1,0:T(8,128)(2,1)S(1)} async-done(((bf16[8,16,4096]{2,1,0:T(8,128)(2,1)}), bf16[8,16,4096]{2,1,0:T(8,128)(2,1)S(1)}, u32[]{:S(2)}, u32[]{:S(2)}) %all-to-all-start) | async-done | bytes 1048608 | tf_op jit(solution)/shard_map/all_to_all | solution.py:249
  39.6 2.5 %shard_map.143 = bf16[4,2,64,128]{3,2,1,0:T(8,128)(2,1)} custom-call(s32[2]{0:T(128)S(1)} %pad_add_fusion.info_ref, bf16[128,4096]{1,0:T(8,128)(2,1)S(1)} %bitcast.23, bf16[64,4096]{1,0:T(8,128)(2,1)} %bitcast.36, bf16[64,4096]{1,0:T(8,128)(2,1)} %collective-permute-done.2.other_ref, f32[2,2,64,128]{3,2,1,0:T(8,128)S(1)} %shard_map.142.table_ref), custom_call_target="tpu_custom_call" | custom-call | flops 2000000000 | bytes 31250000 | tf_op jit(solution)/shard_map/pallas_call | solution.py:214
  42.1 3.3 %all-to-all-start.1 = ((bf16[4,2,64,128]{3,2,1,0:T(8,128)(2,1)}), bf16[4,2,64,128]{3,2,1,0:T(8,128)(2,1)S(1)}, u32[]{:S(2)}, u32[]{:S(2)}) async-start(bf16[4,2,64,128]{3,2,1,0:T(8,128)(2,1)} %shard_map.143), calls=%async_computation.1 | async-start | bytes 262144 | tf_op jit(solution)/shard_map/all_to_all | solution.py:275
  46.0 4.0 %shard_map.144.q_hbm = bf16[2,256,128]{2,1,0:T(8,128)(2,1)} custom-call(bf16[128,4096]{1,0:T(8,128)(2,1)S(1)} %bitcast.24, bf16[4096,256]{1,0:T(8,128)(2,1)} %bitcast.26, bf16[4096,256]{1,0:T(8,128)(2,1)} %collective-permute-done.3.other_hbm, f32[2,2,64,128]{3,2,1,0:T(8,128)S(1)} %shard_map.142.table_ref), custom_call_target="tpu_custom_call" | custom-call | flops 536870912 | bytes 8388608 | tf_op jit(solution)/shard_map/pallas_call | solution.py:214
  50.1 4.4 %shard_map.145 = bf16[8,8,4096]{2,1,0:T(8,128)(2,1)} custom-call(s32[2]{0:T(128)S(1)} %pad_add_fusion.info_ref, s32[1,1]{1,0:T(1,128)} %bitcast.18.length_ref, bf16[4,2,64,128]{3,2,1,0:T(8,128)(2,1)S(1)} %all-to-all-done.1.kv_ref, bf16[256,4096]{1,0:T(8,128)(2,1)S(1)} %bitcast.21, bf16[2,256,128]{2,1,0:T(8,128)(2,1)} %shard_map.144.q_hbm, ...), custom_call_target="tpu_custom_call" | custom-call | flops 469762048 | bytes 7340032 | tf_op jit(solution)/shard_map/pallas_call | solution.py:214
  54.5 6.0 %all-to-all-start.2 = ((bf16[8,8,4096]{2,1,0:T(8,128)(2,1)}), bf16[8,8,4096]{2,1,0:T(8,128)(2,1)S(1)}, u32[]{:S(2)}, u32[]{:S(2)}) async-start(bf16[8,8,4096]{2,1,0:T(8,128)(2,1)} %shard_map.145), calls=%async_computation.2 | async-start | bytes 1048576 | tf_op jit(solution)/shard_map/all_to_all | solution.py:306
  60.5 4.4 %shard_map.146 = bf16[8,8,4096]{2,1,0:T(8,128)(2,1)} custom-call(s32[2]{0:T(128)S(1)} %pad_add_fusion.info_ref, s32[1,1]{1,0:T(1,128)} %bitcast.19.length_ref, bf16[4,2,64,128]{3,2,1,0:T(8,128)(2,1)S(1)} %all-to-all-done.1.kv_ref, bf16[256,4096]{1,0:T(8,128)(2,1)S(1)} %bitcast.22, bf16[2,256,128]{2,1,0:T(8,128)(2,1)} %shard_map.144.q_hbm, ...), custom_call_target="tpu_custom_call" | custom-call | flops 469762048 | bytes 7340032 | tf_op jit(solution)/shard_map/pallas_call | solution.py:214
  64.9 4.0 %all-to-all-done.2 = bf16[8,8,4096]{2,1,0:T(8,128)(2,1)S(1)} async-done(((bf16[8,8,4096]{2,1,0:T(8,128)(2,1)}), bf16[8,8,4096]{2,1,0:T(8,128)(2,1)S(1)}, u32[]{:S(2)}, u32[]{:S(2)}) %all-to-all-start.2) | async-done | bytes 524320 | tf_op jit(solution)/shard_map/all_to_all | solution.py:306
  68.9 5.5 %all-to-all-start.3 = ((bf16[8,8,4096]{2,1,0:T(8,128)(2,1)}), bf16[8,8,4096]{2,1,0:T(8,128)(2,1)S(1)}, u32[]{:S(2)}, u32[]{:S(2)}) async-start(bf16[8,8,4096]{2,1,0:T(8,128)(2,1)} %shard_map.146), calls=%async_computation.3 | async-start | bytes 1048576 | tf_op jit(solution)/shard_map/all_to_all | solution.py:306
  74.5 1.9 %collective-permute-start.7 = (bf16[8,4096]{1,0:T(8,128)(2,1)S(1)}, bf16[8,4096]{1,0:T(8,128)(2,1)S(1)}, u32[]{:S(2)}, u32[]{:S(2)}) collective-permute-start(bf16[8,4096]{1,0:T(8,128)(2,1)S(1)} %reduce_sum.24), channel_id=1, source_target_pairs={{0,16},{16,32},{32,48},{48,64},{64,80},{80,96},{96,112},{112,128},... | collective-permute-start | bytes 196616 | tf_op jit(solution)/shard_map/ppermute | solution.py:184
  76.4 5.5 %all-to-all-done.3 = bf16[8,8,4096]{2,1,0:T(8,128)(2,1)S(1)} async-done(((bf16[8,8,4096]{2,1,0:T(8,128)(2,1)}), bf16[8,8,4096]{2,1,0:T(8,128)(2,1)S(1)}, u32[]{:S(2)}, u32[]{:S(2)}) %all-to-all-start.3) | async-done | bytes 524320 | tf_op jit(solution)/shard_map/all_to_all | solution.py:306
  81.9 0.7 reduce_sum.25
  82.6 2.9 %collective-permute-done.7 = bf16[8,4096]{1,0:T(8,128)(2,1)S(1)} collective-permute-done((bf16[8,4096]{1,0:T(8,128)(2,1)S(1)}, bf16[8,4096]{1,0:T(8,128)(2,1)S(1)}, u32[]{:S(2)}, u32[]{:S(2)}) %collective-permute-start.7) | collective-permute-done | bytes 65568 | tf_op jit(solution)/shard_map/ppermute | solution.py:184
  (23 shorter events, 2.2 us)
Async XLA Ops:
  0.6 37.1 %copy-start.1 = (f32[2,64,128]{2,1,0:T(8,128)S(1)}, f32[2,64,128]{2,1,0:T(8,128)}, u32[]{:S(2)}) copy-start(f32[2,64,128]{2,1,0:T(8,128)} %constant.44.clone.cos_tok) | copy-start | bytes 196612
  0.6 37.1 %copy-start.2 = (f32[2,64,128]{2,1,0:T(8,128)S(1)}, f32[2,64,128]{2,1,0:T(8,128)}, u32[]{:S(2)}) copy-start(f32[2,64,128]{2,1,0:T(8,128)} %constant.45.clone.sin_tok) | copy-start | bytes 196612
  0.7 37.1 %copy-start.3 = (f32[64,128]{1,0:T(8,128)S(1)}, f32[64,128]{1,0:T(8,128)}, u32[]{:S(2)}) copy-start(f32[64,128]{1,0:T(8,128)} %constant.46.clone.cos_span) | copy-start | bytes 98308
  0.7 37.1 %copy-start.4 = (f32[64,128]{1,0:T(8,128)S(1)}, f32[64,128]{1,0:T(8,128)}, u32[]{:S(2)}) copy-start(f32[64,128]{1,0:T(8,128)} %constant.47.clone.sin_span) | copy-start | bytes 98308
  0.7 28.3 %copy-start = (bf16[1,256,4096]{2,1,0:T(8,128)(2,1)S(1)}, bf16[1,256,4096]{2,1,0:T(8,128)(2,1)}, u32[]{:S(2)}) copy-start(bf16[1,256,4096]{2,1,0:T(8,128)(2,1)} %param.20) | copy-start | bytes 6291460
  0.7 20.8 %collective-permute-start.1 = (bf16[384,256]{1,0:T(8,128)(2,1)}, bf16[384,256]{1,0:T(8,128)(2,1)S(1)}, u32[]{:S(2)}, u32[]{:S(2)}) collective-permute-start(bf16[384,256]{1,0:T(8,128)(2,1)} %bitcast.27), channel_id=1, source_target_pairs={{0,2},{1,3},{2,0},{3,1},{4,6},{5,7},{6,4},{7,5},{8,10},{9,11},{10,... | collective-permute-start | bytes 589832 | tf_op jit(solution)/shard_map/ppermute | solution.py:179
  6.7 12.8 %collective-permute-start = (bf16[8,4224]{1,0:T(8,128)(2,1)S(1)}, bf16[8,4224]{1,0:T(8,128)(2,1)S(1)}, u32[]{:S(2)}, u32[]{:S(2)}) collective-permute-start(bf16[8,4224]{1,0:T(8,128)(2,1)S(1)} %shard_map.140), channel_id=1, source_target_pairs={{0,16},{16,32},{32,48},{48,64},{64,80},{80,96},{96,112},{112,128},... | collective-permute-start | bytes 202760 | tf_op jit(solution)/shard_map/ppermute | solution.py:184
  21.5 0.7 copy-start.5
  22.2 17.4 %all-to-all-start = ((bf16[8,16,4096]{2,1,0:T(8,128)(2,1)}), bf16[8,16,4096]{2,1,0:T(8,128)(2,1)S(1)}, u32[]{:S(2)}, u32[]{:S(2)}) async-start(bf16[8,16,4096]{2,1,0:T(8,128)(2,1)} %shard_map.141), calls=%async_computation | async-start | bytes 2097152 | tf_op jit(solution)/shard_map/all_to_all | solution.py:249
  27.0 19.0 %collective-permute-start.3 = (bf16[4096,256]{1,0:T(8,128)(2,1)}, bf16[4096,256]{1,0:T(8,128)(2,1)}, u32[]{:S(2)}, u32[]{:S(2)}) collective-permute-start(bf16[4096,256]{1,0:T(8,128)(2,1)} %bitcast.25), channel_id=1, source_target_pairs={{0,1},{1,0},{2,3},{3,2},{4,5},{5,4},{6,7},{7,6},{8,9},{9,8},{10,11... | collective-permute-start | bytes 6291464 | tf_op jit(solution)/shard_map/ppermute | solution.py:179
  29.0 21.1 %collective-permute-start.6 = (bf16[256,4096]{1,0:T(8,128)(2,1)S(1)}, bf16[256,4096]{1,0:T(8,128)(2,1)}, u32[]{:S(2)}, u32[]{:S(2)}) collective-permute-start(bf16[256,4096]{1,0:T(8,128)(2,1)S(1)} %bitcast.20), channel_id=1, source_target_pairs={{0,1},{1,0},{2,3},{3,2},{4,5},{5,4},{6,7},{7,6},{8,9},{9,8},{10,11... | collective-permute-start | bytes 6291464 | tf_op jit(solution)/shard_map/ppermute | solution.py:179
  31.4 7.1 %collective-permute-start.2 = (bf16[64,4096]{1,0:T(8,128)(2,1)}, bf16[64,4096]{1,0:T(8,128)(2,1)}, u32[]{:S(2)}, u32[]{:S(2)}) collective-permute-start(bf16[64,4096]{1,0:T(8,128)(2,1)} %bitcast.35), channel_id=1, source_target_pairs={{0,1},{1,0},{2,3},{3,2},{4,5},{5,4},{6,7},{7,6},{8,9},{9,8},{10,11... | collective-permute-start | bytes 1572872 | tf_op jit(solution)/shard_map/ppermute | solution.py:179
  33.4 16.6 %collective-permute-start.4 = (bf16[384,256]{1,0:T(8,128)(2,1)}, bf16[384,256]{1,0:T(8,128)(2,1)}, u32[]{:S(2)}, u32[]{:S(2)}) collective-permute-start(bf16[384,256]{1,0:T(8,128)(2,1)} %bitcast.28), channel_id=1, source_target_pairs={{0,1},{1,0},{2,3},{3,2},{4,5},{5,4},{6,7},{7,6},{8,9},{9,8},{10,11... | collective-permute-start | bytes 589832 | tf_op jit(solution)/shard_map/ppermute | solution.py:179
  35.8 14.2 %collective-permute-start.5 = (bf16[384,256]{1,0:T(8,128)(2,1)}, bf16[384,256]{1,0:T(8,128)(2,1)}, u32[]{:S(2)}, u32[]{:S(2)}) collective-permute-start(bf16[384,256]{1,0:T(8,128)(2,1)} %copy-done.5), channel_id=1, source_target_pairs={{0,1},{1,0},{2,3},{3,2},{4,5},{5,4},{6,7},{7,6},{8,9},{9,8},{10,11... | collective-permute-start | bytes 589832 | tf_op jit(solution)/shard_map/ppermute | solution.py:179
  42.1 8.0 %all-to-all-start.1 = ((bf16[4,2,64,128]{3,2,1,0:T(8,128)(2,1)}), bf16[4,2,64,128]{3,2,1,0:T(8,128)(2,1)S(1)}, u32[]{:S(2)}, u32[]{:S(2)}) async-start(bf16[4,2,64,128]{3,2,1,0:T(8,128)(2,1)} %shard_map.143), calls=%async_computation.1 | async-start | bytes 262144 | tf_op jit(solution)/shard_map/all_to_all | solution.py:275
  54.5 14.4 %all-to-all-start.2 = ((bf16[8,8,4096]{2,1,0:T(8,128)(2,1)}), bf16[8,8,4096]{2,1,0:T(8,128)(2,1)S(1)}, u32[]{:S(2)}, u32[]{:S(2)}) async-start(bf16[8,8,4096]{2,1,0:T(8,128)(2,1)} %shard_map.145), calls=%async_computation.2 | async-start | bytes 1048576 | tf_op jit(solution)/shard_map/all_to_all | solution.py:306
  68.9 13.0 %all-to-all-start.3 = ((bf16[8,8,4096]{2,1,0:T(8,128)(2,1)}), bf16[8,8,4096]{2,1,0:T(8,128)(2,1)S(1)}, u32[]{:S(2)}, u32[]{:S(2)}) async-start(bf16[8,8,4096]{2,1,0:T(8,128)(2,1)} %shard_map.146), calls=%async_computation.3 | async-start | bytes 1048576 | tf_op jit(solution)/shard_map/all_to_all | solution.py:306
  74.5 11.1 %collective-permute-start.7 = (bf16[8,4096]{1,0:T(8,128)(2,1)S(1)}, bf16[8,4096]{1,0:T(8,128)(2,1)S(1)}, u32[]{:S(2)}, u32[]{:S(2)}) collective-permute-start(bf16[8,4096]{1,0:T(8,128)(2,1)S(1)} %reduce_sum.24), channel_id=1, source_target_pairs={{0,16},{16,32},{32,48},{48,64},{64,80},{80,96},{96,112},{112,128},... | collective-permute-start | bytes 196616 | tf_op jit(solution)/shard_map/ppermute | solution.py:184

commit v4 on v3

--- a/solution.py
+++ b/solution.py
@@ -54,7 +54,10 @@
         out_ref[copy] = normed
 
 
-def table_kernel(info_ref, span_ref, earlier_ref, cos_tok, sin_tok, cos_span, sin_span, out_ref):
+def table_kernel(
+    info_ref, span_ref, length_ref, earlier_ref, cos_tok, sin_tok, cos_span, sin_span, out_ref, slots_ref
+):
+    slots_ref[...] = jnp.broadcast_to(length_ref[...], slots_ref.shape)
     core = info_ref[0]
     late = earlier_ref[:, -HD:].astype(jnp.float32)[:1].astype(jnp.int32)
     spans = lax.broadcasted_iota(jnp.int32, cos_span.shape, 0)
@@ -81,26 +84,33 @@
 
 
 def query_kernel(rows_ref, own_hbm, other_hbm, table_ref, q_ref, weight_ref, sems):
-    slices = []
+    sides, steps = sems.shape
+    depth = weight_ref.shape[1] // steps
+    copies = []
     for side, weight_hbm in enumerate((own_hbm, other_hbm)):
-        for head in range(weight_hbm.shape[1] // HD):
-            columns = pl.ds(head * HD, HD)
-            at = len(slices)
-            slices.append(
+        for step in range(steps):
+            part = pl.ds(step * depth, depth)
+            copies.append(
                 pltpu.make_async_copy(
-                    weight_hbm.at[:, columns], weight_ref.at[side, :, columns], sems.at[at]
+                    weight_hbm.at[part], weight_ref.at[side, part], sems.at[side, step]
                 )
             )
-            slices[at].start()
+            copies[-1].start()
     rows = rows_ref.shape[0] // 2
-    heads = len(slices) // 2
-    for at in range(len(slices)):
-        slices[at].wait()
-        weight = weight_ref[at // heads, :, at % heads * HD : (at % heads + 1) * HD]
-        queries = jnp.dot(rows_ref[...], weight, preferred_element_type=jnp.float32)
+    for side in range(sides):
+        queries = 0.0
+        for step in range(steps):
+            part = pl.ds(step * depth, depth)
+            copies[side * steps + step].wait()
+            queries += jnp.dot(
+                rows_ref[:, part], weight_ref[side, part], preferred_element_type=jnp.float32
+            )
+        heads = queries.shape[1] // HD
         for tick in range(2):
-            values = of_tick(queries, tick)
-            q_ref[tick, pl.ds(at * rows, rows), :] = rotated(values, table_ref, tick)
+            for head in range(heads):
+                values = of_tick(queries[:, head * HD : (head + 1) * HD], tick)
+                there = pl.ds((side * heads + head) * rows, rows)
+                q_ref[tick, there, :] = rotated(values, table_ref, tick)
 
 
 def pair_kernel(info_ref, rows_ref, own_ref, other_ref, table_ref, kv_ref):
@@ -118,13 +128,16 @@
 
 
 def attend_kernel(
-    info_ref, length_ref, kv_ref, wout_own, q_hbm, own, from_z, from_core, from_both, wout_hbm,
-    out_ref, q_ref, cache_ref, wout_other, sems, *, tick,
+    info_ref, slots_ref, kv_ref, wout_own, q_hbm, own, from_z, from_core, from_both, wout_hbm,
+    out_hbm, q_ref, cache_ref, wout_other, out_ref, sems, out_sems, *, tick,
 ):
     copies = [pltpu.make_async_copy(q_hbm.at[tick], q_ref, sems.at[0])]
     for at, cache in enumerate((own, from_z, from_core, from_both)):
         copies.append(pltpu.make_async_copy(cache, cache_ref.at[at], sems.at[1 + at]))
-    copies.append(pltpu.make_async_copy(wout_hbm, wout_other, sems.at[5]))
+    depth = wout_other.shape[0] // 4
+    for at in range(4):
+        part = pl.ds(at * depth, depth)
+        copies.append(pltpu.make_async_copy(wout_hbm.at[part], wout_other.at[part], sems.at[5 + at]))
     for copy in copies:
         copy.start()
     for copy in copies[:5]:
@@ -148,7 +161,7 @@
     for at, (z, c) in enumerate(places):
         keys.append(cache_ref[at, :, :HD])
         values.append(cache_ref[at, :, HD:])
-        allowed.append((z * 2 + c) * block + slot < length_ref[...])
+        allowed.append((z * 2 + c) * block + slot < slots_ref[:1, :1])
 
     scores = []
     for key, seen in zip(keys, allowed):
@@ -164,15 +177,26 @@
     heads = [result[at : at + rows] for at in range(0, queries.shape[0], rows)]
     half = len(heads) // 2
     sides = [jnp.concatenate(heads[:half], axis=1), jnp.concatenate(heads[half:], axis=1)]
-    copies[5].wait()
-    step = 1024
-    for left in range(0, width, step):
-        columns = pl.ds(left, step)
+    for copy in copies[5:]:
+        copy.wait()
+    steps = out_sems.shape[0]
+    step = width // steps
+    out_copies = []
+    for at in range(steps):
+        columns = pl.ds(at * step, step)
         part = sum(
             jnp.dot(side, wout_ref[:, columns], preferred_element_type=jnp.float32)
             for side, wout_ref in zip(sides, (wout_own, wout_other))
         )
         out_ref[:, :, columns] = part.reshape(chips, tokens, step).astype(jnp.bfloat16)
+        out_copies.append(
+            pltpu.make_async_copy(
+                out_ref.at[:, :, columns], out_hbm.at[:, :, columns], out_sems.at[at]
+            )
+        )
+        out_copies[at].start()
+    for copy in out_copies:
+        copy.wait()
 
 
 def swapped(array, bit):
@@ -209,14 +233,14 @@
         place = place or (0,) * len(shape)
         return pl.BlockSpec(shape, lambda step: place)
 
-    def kernel(body, inputs, outs, limit, flops=1 << 20, specs=None, scratch=()):
+    def kernel(body, inputs, outs, limit, flops=1 << 20, specs=None, scratch=(), places=None):
         specs = specs or [smem if a.ndim == 1 else block(a.shape) for a in inputs]
         return pl.pallas_call(
             body,
             grid=(1,),
             out_shape=outs,
             in_specs=specs,
-            out_specs=[block(out.shape) for out in outs],
+            out_specs=places or [block(out.shape) for out in outs],
             scratch_shapes=scratch,
             compiler_params=pltpu.CompilerParams(vmem_limit_bytes=limit * MIB),
             cost_estimate=pl.CostEstimate(
@@ -244,16 +268,18 @@
         [in_hbm(residual[0]), in_vmem(earlier), in_hbm(norm_gain)],
         [pltpu.HBM((chips, 2 * tokens, width), bf16)],
         16,
+        10 * 10**9,
     )
     normed, cache_z = after(normed, cache_z)
     gathered = lax.all_to_all(normed, "tp", 0, 0, axis_index_groups=same_core)
     gathered = gathered.reshape(2 * rows, width)
 
     _, late_earlier = after(normed, earlier)
-    (table,) = kernel(
+    table, slots = kernel(
         table_kernel,
-        [info, span, late_earlier, cos_tok, sin_tok, cos_span, sin_span],
-        [jax.ShapeDtypeStruct((2, 2, rows, HD), f32)],
+        [info, span, length, late_earlier]
+        + [in_hbm(constant) for constant in (cos_tok, sin_tok, cos_span, sin_span)],
+        [jax.ShapeDtypeStruct((2, 2, rows, HD), f32), jax.ShapeDtypeStruct((8, HD), jnp.int32)],
         16,
         flops=0,
     )
@@ -281,7 +307,7 @@
         24,
         4 * rows * heads * HD * width,
         [block(gathered.shape), anywhere, anywhere, block(table.shape)],
-        [pltpu.VMEM((2, *own_w_query.shape), bf16), pltpu.SemaphoreType.DMA((heads,))],
+        [pltpu.VMEM((2, *own_w_query.shape), bf16), pltpu.SemaphoreType.DMA((2, 4))],
     )
 
     def partial_output(tick):
@@ -289,17 +315,20 @@
         far = [in_hbm(array) for array in (queries, *caches, other_w_out)]
         return kernel(
             functools.partial(attend_kernel, tick=tick),
-            [info, length, pairs, own_w_out, *far],
+            [info, slots, pairs, own_w_out, *far],
             [pltpu.HBM((chips, tokens, width), bf16)],
             24,
             2 * rows * heads * HD * (width + 2 * PREFIX),
-            [smem, block(length.shape), pair, block(own_w_out.shape)] + [anywhere] * 6,
+            [smem, block(slots.shape), pair, block(own_w_out.shape)] + [anywhere] * 6,
             [
                 pltpu.VMEM((heads * rows, HD), bf16),
                 pltpu.VMEM((4, *cache_own.shape), bf16),
                 pltpu.VMEM(own_w_out.shape, bf16),
-                pltpu.SemaphoreType.DMA((6,)),
+                pltpu.VMEM((chips, tokens, width), bf16),
+                pltpu.SemaphoreType.DMA((9,)),
+                pltpu.SemaphoreType.DMA((4,)),
             ],
+            [anywhere],
         )[0]
 
     def collected(partial):

time: 87 us -> 84.4 us (0.970)
  waiting for transfers between devices: 20.3 us -> 15.3 us
  starting transfers between devices: 42.6 us -> 46 us
    all_to_all x2, waiting for transfers between devices: 9.54 us -> 6.58 us  [collected(): partial = lax.all_to_all(partial, 'tp', 0, 0, axis_index_groups=same_core)]
    ppermute x2, starting transfers between devices: 8.01 us -> 10.5 us  [to_next_section(): lax.ppermute(array, 'segment', [(i, i + 1) for i in range(sections - 1)])]
    ppermute x2, waiting for transfers between devices: 9.61 us -> 7.11 us  [to_next_section(): lax.ppermute(array, 'segment', [(i, i + 1) for i in range(sections - 1)])]
    all_to_all x1, starting transfers between devices: 4.83 us -> 6.35 us  [shards(): gathered = lax.all_to_all(normed, 'tp', 0, 0, axis_index_groups=same_core)]
    all_to_all x1, waiting for transfers between devices: 0.01 us -> 0.9 us  [shards(): pairs = lax.all_to_all(pairs, 'tp', 0, 0, axis_index_groups=same_head)]
  transfers between devices with their start and end apart: 12 -> 12, of which waited for: 5 -> 6; matrix products, arithmetic and copies ran while one was open for 1% -> 1% of each run, Pallas kernels for 17% -> 16%
where the time goes in v4:
time: 84.4 us; the launch traced here: 83.5 us
  starting transfers between devices  46 us (55%)
  Pallas kernels  18.7 us (22%)
  waiting for transfers between devices  15.3 us (18%)
  between operations  2.11 us (2%)
  other arithmetic  1.5 us (2%)
    pallas_call x7, Pallas kernels, kernel(): pl.pallas_call(body, grid=(1,), out_shape=outs, in_specs=specs, out_specs...  18.7 us
    ppermute x6, starting transfers between devices, swapped(): lax.ppermute(array, 'tp', [(i, i ^ bit) for i in range(lax.axis_size('tp'...  14.8 us
    all_to_all x2, starting transfers between devices, collected(): partial = lax.all_to_all(partial, 'tp', 0, 0, axis_index_groups=same_core)  11 us
    ppermute x2, starting transfers between devices, to_next_section(): lax.ppermute(array, 'segment', [(i, i + 1) for i in range(sections - 1)])  10.5 us
    ppermute x2, waiting for transfers between devices, to_next_section(): lax.ppermute(array, 'segment', [(i, i + 1) for i in range(sections - 1)])  7.11 us
    all_to_all x2, waiting for transfers between devices, collected(): partial = lax.all_to_all(partial, 'tp', 0, 0, axis_index_groups=same_core)  6.58 us
    all_to_all x1, starting transfers between devices, shards(): gathered = lax.all_to_all(normed, 'tp', 0, 0, axis_index_groups=same_core)  6.35 us
    all_to_all x1, starting transfers between devices, shards(): pairs = lax.all_to_all(pairs, 'tp', 0, 0, axis_index_groups=same_head)  3.32 us
  transfers between devices with their start and end apart: 12, of which 6 were waited for; matrix products, arithmetic and copies ran while one was open for 1% of the time, Pallas kernels for 16%

profile of v4, /device:TPU:34, one launch (start us, length us, event | category | flops | bytes accessed | tf_op | source)
XLA Modules:
  0.0 83.5 jit_solution(634227976303094826)
XLA Ops:
  1.3 0.9 %shard_map.140 = bf16[8,4224]{1,0:T(8,128)(2,1)S(1)} custom-call(s32[1,1]{1,0:T(1,128)} %bitcast.16.span_ref, bf16[8,4096]{1,0:T(8,128)(2,1)} %bitcast.27, bf16[8,4096]{1,0:T(8,128)(2,1)} %bitcast.26), custom_call_target="tpu_custom_call" | custom-call | flops 1048576 | bytes 16384 | tf_op jit(solution)/shard_map/pallas_call | solution.py:238
  2.2 6.1 %collective-permute-start = (bf16[8,4224]{1,0:T(8,128)(2,1)S(1)}, bf16[8,4224]{1,0:T(8,128)(2,1)S(1)}, u32[]{:S(2)}, u32[]{:S(2)}) collective-permute-start(bf16[8,4224]{1,0:T(8,128)(2,1)S(1)} %shard_map.140), channel_id=1, source_target_pairs={{0,16},{16,32},{32,48},{48,64},{64,80},{80,96},{96,112},{112,128},... | collective-permute-start | bytes 202760 | tf_op jit(solution)/shard_map/ppermute | solution.py:208
  8.3 4.3 %collective-permute-start.1 = (bf16[384,256]{1,0:T(8,128)(2,1)}, bf16[384,256]{1,0:T(8,128)(2,1)}, u32[]{:S(2)}, u32[]{:S(2)}) collective-permute-start(bf16[384,256]{1,0:T(8,128)(2,1)} %bitcast.6.own), channel_id=1, source_target_pairs={{0,2},{1,3},{2,0},{3,1},{4,6},{5,7},{6,4},{7,5},{8,10},{9,11},{10,... | collective-permute-start | bytes 589832 | tf_op jit(solution)/shard_map/ppermute | solution.py:203
  12.6 4.0 %collective-permute-done.earlier_ref = bf16[8,4224]{1,0:T(8,128)(2,1)S(1)} collective-permute-done((bf16[8,4224]{1,0:T(8,128)(2,1)S(1)}, bf16[8,4224]{1,0:T(8,128)(2,1)S(1)}, u32[]{:S(2)}, u32[]{:S(2)}) %collective-permute-start) | collective-permute-done | bytes 67616 | tf_op jit(solution)/shard_map/ppermute | solution.py:208
  16.6 2.0 %shard_map.141 = bf16[8,16,4096]{2,1,0:T(8,128)(2,1)} custom-call(bf16[8,4096]{1,0:T(8,128)(2,1)} %bitcast.28, bf16[8,4224]{1,0:T(8,128)(2,1)S(1)} %collective-permute-done.earlier_ref, bf16[1,4096]{1,0:T(2,128)(2,1)} %gain_ref.1), custom_call_target="tpu_custom_call" | custom-call | flops 10000000000 | bytes 156250000 | tf_op jit(solution)/shard_map/pallas_call | solution.py:238
  18.6 6.4 %all-to-all-start = ((bf16[8,16,4096]{2,1,0:T(8,128)(2,1)}), bf16[8,16,4096]{2,1,0:T(8,128)(2,1)S(1)}, u32[]{:S(2)}, u32[]{:S(2)}) async-start(bf16[8,16,4096]{2,1,0:T(8,128)(2,1)} %shard_map.141), calls=%async_computation | async-start | bytes 2097152 | tf_op jit(solution)/shard_map/all_to_all | solution.py:274
  25.0 1.9 %collective-permute-start.3 = (bf16[4096,256]{1,0:T(8,128)(2,1)}, bf16[4096,256]{1,0:T(8,128)(2,1)}, u32[]{:S(2)}, u32[]{:S(2)}) collective-permute-start(bf16[4096,256]{1,0:T(8,128)(2,1)} %bitcast.24), channel_id=1, source_target_pairs={{0,1},{1,0},{2,3},{3,2},{4,5},{5,4},{6,7},{7,6},{8,9},{9,8},{10,11... | collective-permute-start | bytes 6291464 | tf_op jit(solution)/shard_map/ppermute | solution.py:203
  26.9 2.4 %collective-permute-start.6 = (bf16[256,4096]{1,0:T(8,128)(2,1)S(1)}, bf16[256,4096]{1,0:T(8,128)(2,1)}, u32[]{:S(2)}, u32[]{:S(2)}) collective-permute-start(bf16[256,4096]{1,0:T(8,128)(2,1)S(1)} %bitcast.19), channel_id=1, source_target_pairs={{0,1},{1,0},{2,3},{3,2},{4,5},{5,4},{6,7},{7,6},{8,9},{9,8},{10,11... | collective-permute-start | bytes 6291464 | tf_op jit(solution)/shard_map/ppermute | solution.py:203
  29.3 1.9 %collective-permute-start.2 = (bf16[64,4096]{1,0:T(8,128)(2,1)}, bf16[64,4096]{1,0:T(8,128)(2,1)}, u32[]{:S(2)}, u32[]{:S(2)}) collective-permute-start(bf16[64,4096]{1,0:T(8,128)(2,1)} %bitcast.30), channel_id=1, source_target_pairs={{0,1},{1,0},{2,3},{3,2},{4,5},{5,4},{6,7},{7,6},{8,9},{9,8},{10,11... | collective-permute-start | bytes 1572872 | tf_op jit(solution)/shard_map/ppermute | solution.py:203
  32.0 2.4 %collective-permute-start.4 = (bf16[384,256]{1,0:T(8,128)(2,1)}, bf16[384,256]{1,0:T(8,128)(2,1)}, u32[]{:S(2)}, u32[]{:S(2)}) collective-permute-start(bf16[384,256]{1,0:T(8,128)(2,1)} %bitcast.6.own), channel_id=1, source_target_pairs={{0,1},{1,0},{2,3},{3,2},{4,5},{5,4},{6,7},{7,6},{8,9},{9,8},{10,11... | collective-permute-start | bytes 589832 | tf_op jit(solution)/shard_map/ppermute | solution.py:203
  34.4 1.9 %collective-permute-start.5 = (bf16[384,256]{1,0:T(8,128)(2,1)}, bf16[384,256]{1,0:T(8,128)(2,1)}, u32[]{:S(2)}, u32[]{:S(2)}) collective-permute-start(bf16[384,256]{1,0:T(8,128)(2,1)} %collective-permute-done.1.from_z), channel_id=1, source_target_pairs={{0,1},{1,0},{2,3},{3,2},{4,5},{5,4},{6,7},{7,6},{8,9},{9,8},{10,11... | collective-permute-start | bytes 589832 | tf_op jit(solution)/shard_map/ppermute | solution.py:203
  36.3 1.0 %shard_map.142 = (f32[2,2,64,128]{3,2,1,0:T(8,128)S(1)}, s32[8,128]{1,0:T(8,128)S(1)}) custom-call(s32[2]{0:T(128)S(1)} %pad_add_fusion.info_ref, s32[1,1]{1,0:T(1,128)} %bitcast.17.span_ref, s32[1,1]{1,0:T(1,128)} %bitcast.18.length_ref, bf16[8,4224]{1,0:T(8,128)(2,1)S(1)} %collective-permute-done.earlier_ref, f32[2,64,128]{2,1,0:T(8,128)} %constant.44.clone.cos_tok, ...), custom_call_target="tpu_custom_call" | custom-call | tf_op jit(solution)/shard_map/pallas_call | solution.py:238
  38.0 2.5 %shard_map.143 = bf16[4,2,64,128]{3,2,1,0:T(8,128)(2,1)} custom-call(s32[2]{0:T(128)S(1)} %pad_add_fusion.info_ref, bf16[128,4096]{1,0:T(8,128)(2,1)S(1)} %bitcast.22, bf16[64,4096]{1,0:T(8,128)(2,1)} %bitcast.31, bf16[64,4096]{1,0:T(8,128)(2,1)} %collective-permute-done.2.other_ref, f32[2,2,64,128]{3,2,1,0:T(8,128)S(1)} %get-tuple-element.17.table_ref), custom_call_target="tpu_custom_call" | custom-call | flops 2000000000 | bytes 31250000 | tf_op jit(solution)/shard_map/pallas_call | solution.py:238
  40.5 3.3 %all-to-all-start.1 = ((bf16[4,2,64,128]{3,2,1,0:T(8,128)(2,1)}), bf16[4,2,64,128]{3,2,1,0:T(8,128)(2,1)S(1)}, u32[]{:S(2)}, u32[]{:S(2)}) async-start(bf16[4,2,64,128]{3,2,1,0:T(8,128)(2,1)} %shard_map.143), calls=%async_computation.1 | async-start | bytes 262144 | tf_op jit(solution)/shard_map/all_to_all | solution.py:301
  43.8 3.7 %shard_map.144.q_hbm = bf16[2,256,128]{2,1,0:T(8,128)(2,1)} custom-call(bf16[128,4096]{1,0:T(8,128)(2,1)S(1)} %bitcast.23, bf16[4096,256]{1,0:T(8,128)(2,1)} %bitcast.25, bf16[4096,256]{1,0:T(8,128)(2,1)} %collective-permute-done.3.other_hbm, f32[2,2,64,128]{3,2,1,0:T(8,128)S(1)} %get-tuple-element.17.table_ref), custom_call_target="tpu_custom_call" | custom-call | flops 536870912 | bytes 8388608 | tf_op jit(solution)/shard_map/pallas_call | solution.py:238
  47.5 0.9 %all-to-all-done.1.kv_ref = bf16[4,2,64,128]{3,2,1,0:T(8,128)(2,1)S(1)} async-done(((bf16[4,2,64,128]{3,2,1,0:T(8,128)(2,1)}), bf16[4,2,64,128]{3,2,1,0:T(8,128)(2,1)S(1)}, u32[]{:S(2)}, u32[]{:S(2)}) %all-to-all-start.1) | async-done | bytes 131104 | tf_op jit(solution)/shard_map/all_to_all | solution.py:301
  48.4 4.3 %shard_map.145 = bf16[8,8,4096]{2,1,0:T(8,128)(2,1)} custom-call(s32[2]{0:T(128)S(1)} %pad_add_fusion.info_ref, s32[8,128]{1,0:T(8,128)S(1)} %get-tuple-element.14.slots_ref, bf16[4,2,64,128]{3,2,1,0:T(8,128)(2,1)S(1)} %all-to-all-done.1.kv_ref, bf16[256,4096]{1,0:T(8,128)(2,1)S(1)} %bitcast.20, bf16[2,256,128]{2,1,0:T(8,128)(2,1)} %shard_map.144.q_hbm, ...), custom_call_target="tpu_custom_call" | custom-call | flops 469762048 | bytes 7340032 | tf_op jit(solution)/shard_map/pallas_call | solution.py:238
  52.7 5.5 %all-to-all-start.2 = ((bf16[8,8,4096]{2,1,0:T(8,128)(2,1)}), bf16[8,8,4096]{2,1,0:T(8,128)(2,1)S(1)}, u32[]{:S(2)}, u32[]{:S(2)}) async-start(bf16[8,8,4096]{2,1,0:T(8,128)(2,1)} %shard_map.145), calls=%async_computation.2 | async-start | bytes 1048576 | tf_op jit(solution)/shard_map/all_to_all | solution.py:335
  58.2 4.3 %shard_map.146 = bf16[8,8,4096]{2,1,0:T(8,128)(2,1)} custom-call(s32[2]{0:T(128)S(1)} %pad_add_fusion.info_ref, s32[8,128]{1,0:T(8,128)S(1)} %get-tuple-element.14.slots_ref, bf16[4,2,64,128]{3,2,1,0:T(8,128)(2,1)S(1)} %all-to-all-done.1.kv_ref, bf16[256,4096]{1,0:T(8,128)(2,1)S(1)} %bitcast.21, bf16[2,256,128]{2,1,0:T(8,128)(2,1)} %shard_map.144.q_hbm, ...), custom_call_target="tpu_custom_call" | custom-call | flops 469762048 | bytes 7340032 | tf_op jit(solution)/shard_map/pallas_call | solution.py:238
  62.5 3.7 %all-to-all-done.2 = bf16[8,8,4096]{2,1,0:T(8,128)(2,1)S(1)} async-done(((bf16[8,8,4096]{2,1,0:T(8,128)(2,1)}), bf16[8,8,4096]{2,1,0:T(8,128)(2,1)S(1)}, u32[]{:S(2)}, u32[]{:S(2)}) %all-to-all-start.2) | async-done | bytes 524320 | tf_op jit(solution)/shard_map/all_to_all | solution.py:335
  66.3 5.5 %all-to-all-start.3 = ((bf16[8,8,4096]{2,1,0:T(8,128)(2,1)}), bf16[8,8,4096]{2,1,0:T(8,128)(2,1)S(1)}, u32[]{:S(2)}, u32[]{:S(2)}) async-start(bf16[8,8,4096]{2,1,0:T(8,128)(2,1)} %shard_map.146), calls=%async_computation.3 | async-start | bytes 1048576 | tf_op jit(solution)/shard_map/all_to_all | solution.py:335
  71.8 4.4 %collective-permute-start.7 = (bf16[8,4096]{1,0:T(8,128)(2,1)S(1)}, bf16[8,4096]{1,0:T(8,128)(2,1)S(1)}, u32[]{:S(2)}, u32[]{:S(2)}) collective-permute-start(bf16[8,4096]{1,0:T(8,128)(2,1)S(1)} %reduce_sum.24), channel_id=1, source_target_pairs={{0,16},{16,32},{32,48},{48,64},{64,80},{80,96},{96,112},{112,128},... | collective-permute-start | bytes 196616 | tf_op jit(solution)/shard_map/ppermute | solution.py:208
  76.3 2.8 %all-to-all-done.3 = bf16[8,8,4096]{2,1,0:T(8,128)(2,1)S(1)} async-done(((bf16[8,8,4096]{2,1,0:T(8,128)(2,1)}), bf16[8,8,4096]{2,1,0:T(8,128)(2,1)S(1)}, u32[]{:S(2)}, u32[]{:S(2)}) %all-to-all-start.3) | async-done | bytes 524320 | tf_op jit(solution)/shard_map/all_to_all | solution.py:335
  79.8 3.1 %collective-permute-done.7 = bf16[8,4096]{1,0:T(8,128)(2,1)S(1)} collective-permute-done((bf16[8,4096]{1,0:T(8,128)(2,1)S(1)}, bf16[8,4096]{1,0:T(8,128)(2,1)S(1)}, u32[]{:S(2)}, u32[]{:S(2)}) %collective-permute-start.7) | collective-permute-done | bytes 65568 | tf_op jit(solution)/shard_map/ppermute | solution.py:208
  (13 shorter events, 2.2 us)
Async XLA Ops:
  2.2 14.4 %collective-permute-start = (bf16[8,4224]{1,0:T(8,128)(2,1)S(1)}, bf16[8,4224]{1,0:T(8,128)(2,1)S(1)}, u32[]{:S(2)}, u32[]{:S(2)}) collective-permute-start(bf16[8,4224]{1,0:T(8,128)(2,1)S(1)} %shard_map.140), channel_id=1, source_target_pairs={{0,16},{16,32},{32,48},{48,64},{64,80},{80,96},{96,112},{112,128},... | collective-permute-start | bytes 202760 | tf_op jit(solution)/shard_map/ppermute | solution.py:208
  8.3 10.3 %collective-permute-start.1 = (bf16[384,256]{1,0:T(8,128)(2,1)}, bf16[384,256]{1,0:T(8,128)(2,1)}, u32[]{:S(2)}, u32[]{:S(2)}) collective-permute-start(bf16[384,256]{1,0:T(8,128)(2,1)} %bitcast.6.own), channel_id=1, source_target_pairs={{0,2},{1,3},{2,0},{3,1},{4,6},{5,7},{6,4},{7,5},{8,10},{9,11},{10,... | collective-permute-start | bytes 589832 | tf_op jit(solution)/shard_map/ppermute | solution.py:203
  18.6 8.3 %copy-start = (bf16[1,256,4096]{2,1,0:T(8,128)(2,1)S(1)}, bf16[1,256,4096]{2,1,0:T(8,128)(2,1)}, u32[]{:S(2)}) copy-start(bf16[1,256,4096]{2,1,0:T(8,128)(2,1)} %param.20) | copy-start | bytes 6291460
  18.6 19.4 %all-to-all-start = ((bf16[8,16,4096]{2,1,0:T(8,128)(2,1)}), bf16[8,16,4096]{2,1,0:T(8,128)(2,1)S(1)}, u32[]{:S(2)}, u32[]{:S(2)}) async-start(bf16[8,16,4096]{2,1,0:T(8,128)(2,1)} %shard_map.141), calls=%async_computation | async-start | bytes 2097152 | tf_op jit(solution)/shard_map/all_to_all | solution.py:274
  25.0 18.8 %collective-permute-start.3 = (bf16[4096,256]{1,0:T(8,128)(2,1)}, bf16[4096,256]{1,0:T(8,128)(2,1)}, u32[]{:S(2)}, u32[]{:S(2)}) collective-permute-start(bf16[4096,256]{1,0:T(8,128)(2,1)} %bitcast.24), channel_id=1, source_target_pairs={{0,1},{1,0},{2,3},{3,2},{4,5},{5,4},{6,7},{7,6},{8,9},{9,8},{10,11... | collective-permute-start | bytes 6291464 | tf_op jit(solution)/shard_map/ppermute | solution.py:203
  26.9 21.5 %collective-permute-start.6 = (bf16[256,4096]{1,0:T(8,128)(2,1)S(1)}, bf16[256,4096]{1,0:T(8,128)(2,1)}, u32[]{:S(2)}, u32[]{:S(2)}) collective-permute-start(bf16[256,4096]{1,0:T(8,128)(2,1)S(1)} %bitcast.19), channel_id=1, source_target_pairs={{0,1},{1,0},{2,3},{3,2},{4,5},{5,4},{6,7},{7,6},{8,9},{9,8},{10,11... | collective-permute-start | bytes 6291464 | tf_op jit(solution)/shard_map/ppermute | solution.py:203
  29.3 8.0 %collective-permute-start.2 = (bf16[64,4096]{1,0:T(8,128)(2,1)}, bf16[64,4096]{1,0:T(8,128)(2,1)}, u32[]{:S(2)}, u32[]{:S(2)}) collective-permute-start(bf16[64,4096]{1,0:T(8,128)(2,1)} %bitcast.30), channel_id=1, source_target_pairs={{0,1},{1,0},{2,3},{3,2},{4,5},{5,4},{6,7},{7,6},{8,9},{9,8},{10,11... | collective-permute-start | bytes 1572872 | tf_op jit(solution)/shard_map/ppermute | solution.py:203
  32.0 15.5 %collective-permute-start.4 = (bf16[384,256]{1,0:T(8,128)(2,1)}, bf16[384,256]{1,0:T(8,128)(2,1)}, u32[]{:S(2)}, u32[]{:S(2)}) collective-permute-start(bf16[384,256]{1,0:T(8,128)(2,1)} %bitcast.6.own), channel_id=1, source_target_pairs={{0,1},{1,0},{2,3},{3,2},{4,5},{5,4},{6,7},{7,6},{8,9},{9,8},{10,11... | collective-permute-start | bytes 589832 | tf_op jit(solution)/shard_map/ppermute | solution.py:203
  34.4 13.1 %collective-permute-start.5 = (bf16[384,256]{1,0:T(8,128)(2,1)}, bf16[384,256]{1,0:T(8,128)(2,1)}, u32[]{:S(2)}, u32[]{:S(2)}) collective-permute-start(bf16[384,256]{1,0:T(8,128)(2,1)} %collective-permute-done.1.from_z), channel_id=1, source_target_pairs={{0,1},{1,0},{2,3},{3,2},{4,5},{5,4},{6,7},{7,6},{8,9},{9,8},{10,11... | collective-permute-start | bytes 589832 | tf_op jit(solution)/shard_map/ppermute | solution.py:203
  40.5 7.9 %all-to-all-start.1 = ((bf16[4,2,64,128]{3,2,1,0:T(8,128)(2,1)}), bf16[4,2,64,128]{3,2,1,0:T(8,128)(2,1)S(1)}, u32[]{:S(2)}, u32[]{:S(2)}) async-start(bf16[4,2,64,128]{3,2,1,0:T(8,128)(2,1)} %shard_map.143), calls=%async_computation.1 | async-start | bytes 262144 | tf_op jit(solution)/shard_map/all_to_all | solution.py:301
  52.7 13.5 %all-to-all-start.2 = ((bf16[8,8,4096]{2,1,0:T(8,128)(2,1)}), bf16[8,8,4096]{2,1,0:T(8,128)(2,1)S(1)}, u32[]{:S(2)}, u32[]{:S(2)}) async-start(bf16[8,8,4096]{2,1,0:T(8,128)(2,1)} %shard_map.145), calls=%async_computation.2 | async-start | bytes 1048576 | tf_op jit(solution)/shard_map/all_to_all | solution.py:335
  66.3 12.8 %all-to-all-start.3 = ((bf16[8,8,4096]{2,1,0:T(8,128)(2,1)}), bf16[8,8,4096]{2,1,0:T(8,128)(2,1)S(1)}, u32[]{:S(2)}, u32[]{:S(2)}) async-start(bf16[8,8,4096]{2,1,0:T(8,128)(2,1)} %shard_map.146), calls=%async_computation.3 | async-start | bytes 1048576 | tf_op jit(solution)/shard_map/all_to_all | solution.py:335
  71.8 11.1 %collective-permute-start.7 = (bf16[8,4096]{1,0:T(8,128)(2,1)S(1)}, bf16[8,4096]{1,0:T(8,128)(2,1)S(1)}, u32[]{:S(2)}, u32[]{:S(2)}) collective-permute-start(bf16[8,4096]{1,0:T(8,128)(2,1)S(1)} %reduce_sum.24), channel_id=1, source_target_pairs={{0,16},{16,32},{32,48},{48,64},{64,80},{80,96},{96,112},{112,128},... | collective-permute-start | bytes 196616 | tf_op jit(solution)/shard_map/ppermute | solution.py:208

commit v5 on v4

--- a/solution.py
+++ b/solution.py
@@ -41,14 +41,20 @@
     out_ref[:, width:] = jnp.broadcast_to(index, (tokens, out_ref.shape[1] - width))
 
 
-def normalised(rows_ref, gain_ref):
-    rows = rows_ref[:, : gain_ref.shape[1]].astype(jnp.float32)
+def normalised(rows, gain):
     mean_square = jnp.mean(rows * rows, axis=-1, keepdims=True)
-    return rows * lax.rsqrt(mean_square + norm_eps) * gain_ref[...].astype(jnp.float32)
-
-
-def norm_kernel(residual_ref, earlier_ref, gain_ref, out_ref):
-    ticks = [normalised(ref, gain_ref) for ref in (residual_ref, earlier_ref)]
+    return rows * lax.rsqrt(mean_square + norm_eps) * gain
+
+
+def early_norm_kernel(residual_ref, gain_ref, out_ref, wide_gain_ref):
+    gain = gain_ref[...].astype(jnp.float32)
+    wide_gain_ref[...] = gain
+    out_ref[...] = normalised(residual_ref[...].astype(jnp.float32), gain)
+
+
+def norm_kernel(early_ref, earlier_ref, gain_ref, out_ref):
+    rows = earlier_ref[:, : gain_ref.shape[1]].astype(jnp.float32)
+    ticks = [early_ref[...], normalised(rows, gain_ref[...])]
     normed = jnp.concatenate(ticks, axis=0).astype(jnp.bfloat16)
     for copy in range(out_ref.shape[0]):
         out_ref[copy] = normed
@@ -263,9 +269,15 @@
     )
     earlier = to_next_section(carried)
     cache_z = swapped(prefix_cache[0], 2)
+    early_normed, wide_gain = kernel(
+        early_norm_kernel,
+        [in_hbm(residual[0]), in_hbm(norm_gain)],
+        [pltpu.VMEM((tokens, width), f32), pltpu.VMEM((1, width), f32)],
+        16,
+    )
     (normed,) = kernel(
         norm_kernel,
-        [in_hbm(residual[0]), in_vmem(earlier), in_hbm(norm_gain)],
+        [in_vmem(early_normed), in_vmem(earlier), in_vmem(wide_gain)],
         [pltpu.HBM((chips, 2 * tokens, width), bf16)],
         16,
         10 * 10**9,

time: 84.4 us -> 84.4 us (level)
    ppermute x2, waiting for transfers between devices: 7.11 us -> 6.14 us  [to_next_section(): lax.ppermute(array, 'segment', [(i, i + 1) for i in range(sections - 1)])]
    pallas_call x7 -> x8, Pallas kernels: 18.7 us -> 18.8 us  [kernel(): pl.pallas_call(body, grid=(1,), out_shape=outs, in_specs=specs, out_specs...]
  transfers between devices with their start and end apart: 12 -> 12, of which waited for: 6 -> 7; matrix products, arithmetic and copies ran while one was open for 1% -> 1% of each run, Pallas kernels for 16% -> 16%
where the time goes in v5:
time: 84.4 us; the launch traced here: 83.5 us
  starting transfers between devices  46.4 us (55%)
  Pallas kernels  18.8 us (22%)
  waiting for transfers between devices  14.7 us (17%)
  between operations  2.12 us (3%)
  other arithmetic  1.5 us (2%)
    pallas_call x8, Pallas kernels, kernel(): pl.pallas_call(body, grid=(1,), out_shape=outs, in_specs=specs, out_specs...  18.8 us
    ppermute x6, starting transfers between devices, swapped(): lax.ppermute(array, 'tp', [(i, i ^ bit) for i in range(lax.axis_size('tp'...  14.8 us
    all_to_all x2, starting transfers between devices, collected(): partial = lax.all_to_all(partial, 'tp', 0, 0, axis_index_groups=same_core)  11 us
    ppermute x2, starting transfers between devices, to_next_section(): lax.ppermute(array, 'segment', [(i, i + 1) for i in range(sections - 1)])  10.5 us
    all_to_all x1, starting transfers between devices, shards(): gathered = lax.all_to_all(normed, 'tp', 0, 0, axis_index_groups=same_core)  6.75 us
    all_to_all x2, waiting for transfers between devices, collected(): partial = lax.all_to_all(partial, 'tp', 0, 0, axis_index_groups=same_core)  6.55 us
    ppermute x2, waiting for transfers between devices, to_next_section(): lax.ppermute(array, 'segment', [(i, i + 1) for i in range(sections - 1)])  6.14 us
    all_to_all x1, starting transfers between devices, shards(): pairs = lax.all_to_all(pairs, 'tp', 0, 0, axis_index_groups=same_head)  3.32 us
  transfers between devices with their start and end apart: 12, of which 7 were waited for; matrix products, arithmetic and copies ran while one was open for 1% of the time, Pallas kernels for 16%

profile of v5, /device:TPU:34, one launch (start us, length us, event | category | flops | bytes accessed | tf_op | source)
XLA Modules:
  0.0 83.5 jit_solution(6518914745964520001)
XLA Ops:
  1.3 0.9 %shard_map.140 = bf16[8,4224]{1,0:T(8,128)(2,1)S(1)} custom-call(s32[1,1]{1,0:T(1,128)} %bitcast.16.span_ref, bf16[8,4096]{1,0:T(8,128)(2,1)} %bitcast.26, bf16[8,4096]{1,0:T(8,128)(2,1)} %bitcast.28), custom_call_target="tpu_custom_call" | custom-call | flops 1048576 | bytes 16384 | tf_op jit(solution)/shard_map/pallas_call | solution.py:244
  2.2 6.1 %collective-permute-start = (bf16[8,4224]{1,0:T(8,128)(2,1)S(1)}, bf16[8,4224]{1,0:T(8,128)(2,1)S(1)}, u32[]{:S(2)}, u32[]{:S(2)}) collective-permute-start(bf16[8,4224]{1,0:T(8,128)(2,1)S(1)} %shard_map.140), channel_id=1, source_target_pairs={{0,16},{16,32},{32,48},{48,64},{64,80},{80,96},{96,112},{112,128},... | collective-permute-start | bytes 202760 | tf_op jit(solution)/shard_map/ppermute | solution.py:214
  8.3 4.3 %collective-permute-start.1 = (bf16[384,256]{1,0:T(8,128)(2,1)}, bf16[384,256]{1,0:T(8,128)(2,1)}, u32[]{:S(2)}, u32[]{:S(2)}) collective-permute-start(bf16[384,256]{1,0:T(8,128)(2,1)} %bitcast.6.own), channel_id=1, source_target_pairs={{0,2},{1,3},{2,0},{3,1},{4,6},{5,7},{6,4},{7,5},{8,10},{9,11},{10,... | collective-permute-start | bytes 589832 | tf_op jit(solution)/shard_map/ppermute | solution.py:209
  12.6 1.0 %shard_map.141 = (f32[8,4096]{1,0:T(8,128)S(1)}, f32[1,4096]{1,0:T(1,128)S(1)}) custom-call(bf16[8,4096]{1,0:T(8,128)(2,1)} %bitcast.27, bf16[1,4096]{1,0:T(2,128)(2,1)} %gain_ref.1), custom_call_target="tpu_custom_call" | custom-call | flops 1048576 | bytes 16384 | tf_op jit(solution)/shard_map/pallas_call | solution.py:244
  13.6 3.0 %collective-permute-done.earlier_ref = bf16[8,4224]{1,0:T(8,128)(2,1)S(1)} collective-permute-done((bf16[8,4224]{1,0:T(8,128)(2,1)S(1)}, bf16[8,4224]{1,0:T(8,128)(2,1)S(1)}, u32[]{:S(2)}, u32[]{:S(2)}) %collective-permute-start) | collective-permute-done | bytes 67616 | tf_op jit(solution)/shard_map/ppermute | solution.py:214
  16.6 1.1 %shard_map.142 = bf16[8,16,4096]{2,1,0:T(8,128)(2,1)} custom-call(f32[8,4096]{1,0:T(8,128)S(1)} %get-tuple-element.14.early_ref, bf16[8,4224]{1,0:T(8,128)(2,1)S(1)} %collective-permute-done.earlier_ref, f32[1,4096]{1,0:T(1,128)S(1)} %get-tuple-element.15.gain_ref), custom_call_target="tpu_custom_call" | custom-call | flops 10000000000 | bytes 156250000 | tf_op jit(solution)/shard_map/pallas_call | solution.py:244
  18.2 6.7 %all-to-all-start = ((bf16[8,16,4096]{2,1,0:T(8,128)(2,1)}), bf16[8,16,4096]{2,1,0:T(8,128)(2,1)S(1)}, u32[]{:S(2)}, u32[]{:S(2)}) async-start(bf16[8,16,4096]{2,1,0:T(8,128)(2,1)} %shard_map.142), calls=%async_computation | async-start | bytes 2097152 | tf_op jit(solution)/shard_map/all_to_all | solution.py:286
  25.0 1.9 %collective-permute-start.3 = (bf16[4096,256]{1,0:T(8,128)(2,1)}, bf16[4096,256]{1,0:T(8,128)(2,1)}, u32[]{:S(2)}, u32[]{:S(2)}) collective-permute-start(bf16[4096,256]{1,0:T(8,128)(2,1)} %bitcast.24), channel_id=1, source_target_pairs={{0,1},{1,0},{2,3},{3,2},{4,5},{5,4},{6,7},{7,6},{8,9},{9,8},{10,11... | collective-permute-start | bytes 6291464 | tf_op jit(solution)/shard_map/ppermute | solution.py:209
  26.9 2.4 %collective-permute-start.6 = (bf16[256,4096]{1,0:T(8,128)(2,1)S(1)}, bf16[256,4096]{1,0:T(8,128)(2,1)}, u32[]{:S(2)}, u32[]{:S(2)}) collective-permute-start(bf16[256,4096]{1,0:T(8,128)(2,1)S(1)} %bitcast.19), channel_id=1, source_target_pairs={{0,1},{1,0},{2,3},{3,2},{4,5},{5,4},{6,7},{7,6},{8,9},{9,8},{10,11... | collective-permute-start | bytes 6291464 | tf_op jit(solution)/shard_map/ppermute | solution.py:209
  29.3 1.9 %collective-permute-start.2 = (bf16[64,4096]{1,0:T(8,128)(2,1)}, bf16[64,4096]{1,0:T(8,128)(2,1)}, u32[]{:S(2)}, u32[]{:S(2)}) collective-permute-start(bf16[64,4096]{1,0:T(8,128)(2,1)} %bitcast.30), channel_id=1, source_target_pairs={{0,1},{1,0},{2,3},{3,2},{4,5},{5,4},{6,7},{7,6},{8,9},{9,8},{10,11... | collective-permute-start | bytes 1572872 | tf_op jit(solution)/shard_map/ppermute | solution.py:209
  32.0 2.4 %collective-permute-start.4 = (bf16[384,256]{1,0:T(8,128)(2,1)}, bf16[384,256]{1,0:T(8,128)(2,1)}, u32[]{:S(2)}, u32[]{:S(2)}) collective-permute-start(bf16[384,256]{1,0:T(8,128)(2,1)} %bitcast.6.own), channel_id=1, source_target_pairs={{0,1},{1,0},{2,3},{3,2},{4,5},{5,4},{6,7},{7,6},{8,9},{9,8},{10,11... | collective-permute-start | bytes 589832 | tf_op jit(solution)/shard_map/ppermute | solution.py:209
  34.4 1.9 %collective-permute-start.5 = (bf16[384,256]{1,0:T(8,128)(2,1)}, bf16[384,256]{1,0:T(8,128)(2,1)}, u32[]{:S(2)}, u32[]{:S(2)}) collective-permute-start(bf16[384,256]{1,0:T(8,128)(2,1)} %collective-permute-done.1.from_z), channel_id=1, source_target_pairs={{0,1},{1,0},{2,3},{3,2},{4,5},{5,4},{6,7},{7,6},{8,9},{9,8},{10,11... | collective-permute-start | bytes 589832 | tf_op jit(solution)/shard_map/ppermute | solution.py:209
  36.3 1.0 %shard_map.143 = (f32[2,2,64,128]{3,2,1,0:T(8,128)S(1)}, s32[8,128]{1,0:T(8,128)S(1)}) custom-call(s32[2]{0:T(128)S(1)} %pad_add_fusion.info_ref, s32[1,1]{1,0:T(1,128)} %bitcast.17.span_ref, s32[1,1]{1,0:T(1,128)} %bitcast.18.length_ref, bf16[8,4224]{1,0:T(8,128)(2,1)S(1)} %collective-permute-done.earlier_ref, f32[2,64,128]{2,1,0:T(8,128)} %constant.44.clone.cos_tok, ...), custom_call_target="tpu_custom_call" | custom-call | tf_op jit(solution)/shard_map/pallas_call | solution.py:244
  38.0 2.5 %shard_map.144 = bf16[4,2,64,128]{3,2,1,0:T(8,128)(2,1)} custom-call(s32[2]{0:T(128)S(1)} %pad_add_fusion.info_ref, bf16[128,4096]{1,0:T(8,128)(2,1)S(1)} %bitcast.22, bf16[64,4096]{1,0:T(8,128)(2,1)} %bitcast.31, bf16[64,4096]{1,0:T(8,128)(2,1)} %collective-permute-done.2.other_ref, f32[2,2,64,128]{3,2,1,0:T(8,128)S(1)} %get-tuple-element.21.table_ref), custom_call_target="tpu_custom_call" | custom-call | flops 2000000000 | bytes 31250000 | tf_op jit(solution)/shard_map/pallas_call | solution.py:244
  40.5 3.3 %all-to-all-start.1 = ((bf16[4,2,64,128]{3,2,1,0:T(8,128)(2,1)}), bf16[4,2,64,128]{3,2,1,0:T(8,128)(2,1)S(1)}, u32[]{:S(2)}, u32[]{:S(2)}) async-start(bf16[4,2,64,128]{3,2,1,0:T(8,128)(2,1)} %shard_map.144), calls=%async_computation.1 | async-start | bytes 262144 | tf_op jit(solution)/shard_map/all_to_all | solution.py:313
  43.8 3.6 %shard_map.145.q_hbm = bf16[2,256,128]{2,1,0:T(8,128)(2,1)} custom-call(bf16[128,4096]{1,0:T(8,128)(2,1)S(1)} %bitcast.23, bf16[4096,256]{1,0:T(8,128)(2,1)} %bitcast.25, bf16[4096,256]{1,0:T(8,128)(2,1)} %collective-permute-done.3.other_hbm, f32[2,2,64,128]{3,2,1,0:T(8,128)S(1)} %get-tuple-element.21.table_ref), custom_call_target="tpu_custom_call" | custom-call | flops 536870912 | bytes 8388608 | tf_op jit(solution)/shard_map/pallas_call | solution.py:244
  48.4 4.3 %shard_map.146 = bf16[8,8,4096]{2,1,0:T(8,128)(2,1)} custom-call(s32[2]{0:T(128)S(1)} %pad_add_fusion.info_ref, s32[8,128]{1,0:T(8,128)S(1)} %get-tuple-element.18.slots_ref, bf16[4,2,64,128]{3,2,1,0:T(8,128)(2,1)S(1)} %all-to-all-done.1.kv_ref, bf16[256,4096]{1,0:T(8,128)(2,1)S(1)} %bitcast.20, bf16[2,256,128]{2,1,0:T(8,128)(2,1)} %shard_map.145.q_hbm, ...), custom_call_target="tpu_custom_call" | custom-call | flops 469762048 | bytes 7340032 | tf_op jit(solution)/shard_map/pallas_call | solution.py:244
  52.7 5.5 %all-to-all-start.2 = ((bf16[8,8,4096]{2,1,0:T(8,128)(2,1)}), bf16[8,8,4096]{2,1,0:T(8,128)(2,1)S(1)}, u32[]{:S(2)}, u32[]{:S(2)}) async-start(bf16[8,8,4096]{2,1,0:T(8,128)(2,1)} %shard_map.146), calls=%async_computation.2 | async-start | bytes 1048576 | tf_op jit(solution)/shard_map/all_to_all | solution.py:347
  58.2 4.3 %shard_map.147 = bf16[8,8,4096]{2,1,0:T(8,128)(2,1)} custom-call(s32[2]{0:T(128)S(1)} %pad_add_fusion.info_ref, s32[8,128]{1,0:T(8,128)S(1)} %get-tuple-element.18.slots_ref, bf16[4,2,64,128]{3,2,1,0:T(8,128)(2,1)S(1)} %all-to-all-done.1.kv_ref, bf16[256,4096]{1,0:T(8,128)(2,1)S(1)} %bitcast.21, bf16[2,256,128]{2,1,0:T(8,128)(2,1)} %shard_map.145.q_hbm, ...), custom_call_target="tpu_custom_call" | custom-call | flops 469762048 | bytes 7340032 | tf_op jit(solution)/shard_map/pallas_call | solution.py:244
  62.5 3.7 %all-to-all-done.2 = bf16[8,8,4096]{2,1,0:T(8,128)(2,1)S(1)} async-done(((bf16[8,8,4096]{2,1,0:T(8,128)(2,1)}), bf16[8,8,4096]{2,1,0:T(8,128)(2,1)S(1)}, u32[]{:S(2)}, u32[]{:S(2)}) %all-to-all-start.2) | async-done | bytes 524320 | tf_op jit(solution)/shard_map/all_to_all | solution.py:347
  66.3 5.5 %all-to-all-start.3 = ((bf16[8,8,4096]{2,1,0:T(8,128)(2,1)}), bf16[8,8,4096]{2,1,0:T(8,128)(2,1)S(1)}, u32[]{:S(2)}, u32[]{:S(2)}) async-start(bf16[8,8,4096]{2,1,0:T(8,128)(2,1)} %shard_map.147), calls=%async_computation.3 | async-start | bytes 1048576 | tf_op jit(solution)/shard_map/all_to_all | solution.py:347
  71.8 4.4 %collective-permute-start.7 = (bf16[8,4096]{1,0:T(8,128)(2,1)S(1)}, bf16[8,4096]{1,0:T(8,128)(2,1)S(1)}, u32[]{:S(2)}, u32[]{:S(2)}) collective-permute-start(bf16[8,4096]{1,0:T(8,128)(2,1)S(1)} %reduce_sum.24), channel_id=1, source_target_pairs={{0,16},{16,32},{32,48},{48,64},{64,80},{80,96},{96,112},{112,128},... | collective-permute-start | bytes 196616 | tf_op jit(solution)/shard_map/ppermute | solution.py:214
  76.3 2.8 %all-to-all-done.3 = bf16[8,8,4096]{2,1,0:T(8,128)(2,1)S(1)} async-done(((bf16[8,8,4096]{2,1,0:T(8,128)(2,1)}), bf16[8,8,4096]{2,1,0:T(8,128)(2,1)S(1)}, u32[]{:S(2)}, u32[]{:S(2)}) %all-to-all-start.3) | async-done | bytes 524320 | tf_op jit(solution)/shard_map/all_to_all | solution.py:347
  79.8 3.1 %collective-permute-done.7 = bf16[8,4096]{1,0:T(8,128)(2,1)S(1)} collective-permute-done((bf16[8,4096]{1,0:T(8,128)(2,1)S(1)}, bf16[8,4096]{1,0:T(8,128)(2,1)S(1)}, u32[]{:S(2)}, u32[]{:S(2)}) %collective-permute-start.7) | collective-permute-done | bytes 65568 | tf_op jit(solution)/shard_map/ppermute | solution.py:214
  (14 shorter events, 3.6 us)
Async XLA Ops:
  2.2 14.4 %collective-permute-start = (bf16[8,4224]{1,0:T(8,128)(2,1)S(1)}, bf16[8,4224]{1,0:T(8,128)(2,1)S(1)}, u32[]{:S(2)}, u32[]{:S(2)}) collective-permute-start(bf16[8,4224]{1,0:T(8,128)(2,1)S(1)} %shard_map.140), channel_id=1, source_target_pairs={{0,16},{16,32},{32,48},{48,64},{64,80},{80,96},{96,112},{112,128},... | collective-permute-start | bytes 202760 | tf_op jit(solution)/shard_map/ppermute | solution.py:214
  8.3 9.9 %collective-permute-start.1 = (bf16[384,256]{1,0:T(8,128)(2,1)}, bf16[384,256]{1,0:T(8,128)(2,1)}, u32[]{:S(2)}, u32[]{:S(2)}) collective-permute-start(bf16[384,256]{1,0:T(8,128)(2,1)} %bitcast.6.own), channel_id=1, source_target_pairs={{0,2},{1,3},{2,0},{3,1},{4,6},{5,7},{6,4},{7,5},{8,10},{9,11},{10,... | collective-permute-start | bytes 589832 | tf_op jit(solution)/shard_map/ppermute | solution.py:209
  17.7 9.2 %copy-start = (bf16[1,256,4096]{2,1,0:T(8,128)(2,1)S(1)}, bf16[1,256,4096]{2,1,0:T(8,128)(2,1)}, u32[]{:S(2)}) copy-start(bf16[1,256,4096]{2,1,0:T(8,128)(2,1)} %param.20) | copy-start | bytes 6291460
  18.2 19.8 %all-to-all-start = ((bf16[8,16,4096]{2,1,0:T(8,128)(2,1)}), bf16[8,16,4096]{2,1,0:T(8,128)(2,1)S(1)}, u32[]{:S(2)}, u32[]{:S(2)}) async-start(bf16[8,16,4096]{2,1,0:T(8,128)(2,1)} %shard_map.142), calls=%async_computation | async-start | bytes 2097152 | tf_op jit(solution)/shard_map/all_to_all | solution.py:286
  25.0 18.8 %collective-permute-start.3 = (bf16[4096,256]{1,0:T(8,128)(2,1)}, bf16[4096,256]{1,0:T(8,128)(2,1)}, u32[]{:S(2)}, u32[]{:S(2)}) collective-permute-start(bf16[4096,256]{1,0:T(8,128)(2,1)} %bitcast.24), channel_id=1, source_target_pairs={{0,1},{1,0},{2,3},{3,2},{4,5},{5,4},{6,7},{7,6},{8,9},{9,8},{10,11... | collective-permute-start | bytes 6291464 | tf_op jit(solution)/shard_map/ppermute | solution.py:209
  26.9 21.5 %collective-permute-start.6 = (bf16[256,4096]{1,0:T(8,128)(2,1)S(1)}, bf16[256,4096]{1,0:T(8,128)(2,1)}, u32[]{:S(2)}, u32[]{:S(2)}) collective-permute-start(bf16[256,4096]{1,0:T(8,128)(2,1)S(1)} %bitcast.19), channel_id=1, source_target_pairs={{0,1},{1,0},{2,3},{3,2},{4,5},{5,4},{6,7},{7,6},{8,9},{9,8},{10,11... | collective-permute-start | bytes 6291464 | tf_op jit(solution)/shard_map/ppermute | solution.py:209
  29.3 8.0 %collective-permute-start.2 = (bf16[64,4096]{1,0:T(8,128)(2,1)}, bf16[64,4096]{1,0:T(8,128)(2,1)}, u32[]{:S(2)}, u32[]{:S(2)}) collective-permute-start(bf16[64,4096]{1,0:T(8,128)(2,1)} %bitcast.30), channel_id=1, source_target_pairs={{0,1},{1,0},{2,3},{3,2},{4,5},{5,4},{6,7},{7,6},{8,9},{9,8},{10,11... | collective-permute-start | bytes 1572872 | tf_op jit(solution)/shard_map/ppermute | solution.py:209
  32.0 15.4 %collective-permute-start.4 = (bf16[384,256]{1,0:T(8,128)(2,1)}, bf16[384,256]{1,0:T(8,128)(2,1)}, u32[]{:S(2)}, u32[]{:S(2)}) collective-permute-start(bf16[384,256]{1,0:T(8,128)(2,1)} %bitcast.6.own), channel_id=1, source_target_pairs={{0,1},{1,0},{2,3},{3,2},{4,5},{5,4},{6,7},{7,6},{8,9},{9,8},{10,11... | collective-permute-start | bytes 589832 | tf_op jit(solution)/shard_map/ppermute | solution.py:209
  34.4 13.1 %collective-permute-start.5 = (bf16[384,256]{1,0:T(8,128)(2,1)}, bf16[384,256]{1,0:T(8,128)(2,1)}, u32[]{:S(2)}, u32[]{:S(2)}) collective-permute-start(bf16[384,256]{1,0:T(8,128)(2,1)} %collective-permute-done.1.from_z), channel_id=1, source_target_pairs={{0,1},{1,0},{2,3},{3,2},{4,5},{5,4},{6,7},{7,6},{8,9},{9,8},{10,11... | collective-permute-start | bytes 589832 | tf_op jit(solution)/shard_map/ppermute | solution.py:209
  40.5 7.9 %all-to-all-start.1 = ((bf16[4,2,64,128]{3,2,1,0:T(8,128)(2,1)}), bf16[4,2,64,128]{3,2,1,0:T(8,128)(2,1)S(1)}, u32[]{:S(2)}, u32[]{:S(2)}) async-start(bf16[4,2,64,128]{3,2,1,0:T(8,128)(2,1)} %shard_map.144), calls=%async_computation.1 | async-start | bytes 262144 | tf_op jit(solution)/shard_map/all_to_all | solution.py:313
  52.7 13.5 %all-to-all-start.2 = ((bf16[8,8,4096]{2,1,0:T(8,128)(2,1)}), bf16[8,8,4096]{2,1,0:T(8,128)(2,1)S(1)}, u32[]{:S(2)}, u32[]{:S(2)}) async-start(bf16[8,8,4096]{2,1,0:T(8,128)(2,1)} %shard_map.146), calls=%async_computation.2 | async-start | bytes 1048576 | tf_op jit(solution)/shard_map/all_to_all | solution.py:347
  66.3 12.8 %all-to-all-start.3 = ((bf16[8,8,4096]{2,1,0:T(8,128)(2,1)}), bf16[8,8,4096]{2,1,0:T(8,128)(2,1)S(1)}, u32[]{:S(2)}, u32[]{:S(2)}) async-start(bf16[8,8,4096]{2,1,0:T(8,128)(2,1)} %shard_map.147), calls=%async_computation.3 | async-start | bytes 1048576 | tf_op jit(solution)/shard_map/all_to_all | solution.py:347
  71.8 11.1 %collective-permute-start.7 = (bf16[8,4096]{1,0:T(8,128)(2,1)S(1)}, bf16[8,4096]{1,0:T(8,128)(2,1)S(1)}, u32[]{:S(2)}, u32[]{:S(2)}) collective-permute-start(bf16[8,4096]{1,0:T(8,128)(2,1)S(1)} %reduce_sum.24), channel_id=1, source_target_pairs={{0,16},{16,32},{32,48},{48,64},{64,80},{80,96},{96,112},{112,128},... | collective-permute-start | bytes 196616 | tf_op jit(solution)/shard_map/ppermute | solution.py:214
